TPU v7x, 32 devices: a whole 2x2x4 slice. The times are simulated.
32 devices in a mesh: dp: 32 (over z, y, x, core).
Axes of the slice: x: 2, y: 2, z: 4, core: 2. Of those that a mesh axis runs over, the one named last changes fastest.
Arguments:
- tokens: bfloat16 [16384, 1024], P('dp'), may hold values from -6 to 6
- query_weight: bfloat16 [1024, 1024], P('dp'), may hold values from -0.375 to 0.375
- key_projection_weight: bfloat16 [1024, 512], P('dp'), may hold values from -0.1875 to 0.1875
- value_projection_weight: bfloat16 [1024, 512], P('dp'), may hold values from -0.1875 to 0.1875
- output_weight: bfloat16 [1024, 1024], P(None, 'dp'), may hold values from -1.5 to 1.5
- first_gain: bfloat16 [1024], P('dp'), may hold values from 0.5 to 1.5
- second_gain: bfloat16 [1024], P('dp'), may hold values from 0.5 to 1.5
- router_weight: bfloat16 [1024, 16], P('dp'), may hold values from -0.09375 to 0.09375
- gate_weight: bfloat16 [16, 1024, 512], P(None, 'dp'), may hold values from -0.1875 to 0.1875
- up_weight: bfloat16 [16, 1024, 512], P(None, 'dp'), may hold values from -0.1875 to 0.1875
- down_weight: bfloat16 [16, 512, 1024], P(None, None, 'dp'), may hold values from -0.75 to 0.75
- routes: int32 [16384, 8], P('dp'), may hold values from 0 to 15, all different within a row; in each aligned block of 512 rows (0 to 511, 512 to 1023, ...) at most 288 rows name the same one
- segments: int32 [32, 512], P('dp'), may hold values from 0 to 7, never falling along the last dimension, each value on 1 to 256 neighbouring positions
- cotangent: bfloat16 [16384, 1024], P('dp'), may hold values from -6 to 6
Outputs:
- output: bfloat16 [16384, 1024], P('dp')
- input_grad: float32 [16384, 1024], P('dp')
- query_grad: float32 [1024, 1024], P('dp')
- key_grad: float32 [1024, 512], P('dp')
- value_grad: float32 [1024, 512], P('dp')
- output_weight_grad: float32 [1024, 1024], P(None, 'dp')
- first_gain_grad: float32 [1024], P('dp')
- second_gain_grad: float32 [1024], P('dp')
- router_grad: float32 [1024, 16], P('dp')
- gate_grad: float32 [16, 1024, 512], P(None, 'dp')
- up_grad: float32 [16, 1024, 512], P(None, 'dp')
- down_grad: float32 [16, 512, 1024], P(None, None, 'dp')
Inputs may be any that keep to these rules, and one draw needn't show every extreme that they name: `routes`: each token names 8 different experts; the 512 tokens of one device name no expert more than 288 times, a bound that some block reaches. `segments`: along each sequence the document numbers never fall; each document has 1 to 256 tokens, one exactly 256.
All inputs are finite; a program needn't handle non-finite values.
Results may differ from a plain program's by a relative error of at most 0.013.
The roundings to bfloat16 on the way count: a program that leaves them out, or rounds other values in their place, can miss the bound.
Values may be sent and summed in bfloat16 or wider, within the bound.
No kernel may reach another device: no remote copies, remote signals or barrier semaphores. Data moves between devices by JAX's collectives and lax.ppermute only.
A program may use at most 320 MiB of HBM per device.

v0:
```python
import functools

import jax
import jax.numpy as jnp
from jax import lax
from jax.experimental import pallas as pl
from jax.experimental.pallas import tpu as pltpu
from jax.sharding import PartitionSpec as P

EXPERTS = 16
PLANE = 8
MINE = EXPERTS // PLANE
HEADS = 16
HEAD_SIZE = 64
BLOCK = 128
MOST_DOC = 256
MIB = 2**20
VMEM_ROOM = 60 * MIB
SMALL = pl.CostEstimate(flops=1, bytes_accessed=1, transcendentals=0)
epsilon = 1e-06
neg_large = -1000000000.0
BF = jnp.bfloat16
F32 = jnp.float32


def dot(a, b, ca, cb):
    return lax.dot_general(a, b, (((ca,), (cb,)), ((), ())), preferred_element_type=F32)

def rms_scale(values):
    return lax.rsqrt(jnp.mean(values * values, axis=-1, keepdims=True) + epsilon)

def swap_halves(u):
    lane = lax.broadcasted_iota(jnp.int32, u.shape, 1)
    return jnp.where(lane % 64 < 32, pltpu.roll(u, u.shape[1] - 32, 1), pltpu.roll(u, 32, 1))

def crossed(u, w):
    lane = lax.broadcasted_iota(jnp.int32, u.shape, 1)
    return (
        jnp.where(lane < 64, u, pltpu.roll(w, 64, 1)),
        jnp.where(lane < 64, pltpu.roll(u, 64, 1), w),
    )


def key_range(rows, qb):
    end = (qb + 1) * BLOCK
    return max(0, end - BLOCK - MOST_DOC), end

def fill_mask(mask_ref, seg_col_ref, seg_row_ref, rows):
    for qb in range(rows // BLOCK):
        low, high = key_range(rows, qb)
        keys = low + lax.broadcasted_iota(jnp.int32, (high - low, BLOCK), 0)
        queries = qb * BLOCK + lax.broadcasted_iota(jnp.int32, (high - low, BLOCK), 1)
        same = seg_col_ref[low:high, :1] == seg_row_ref[:1, qb * BLOCK : (qb + 1) * BLOCK]
        mask_ref[qb, : high - low] = jnp.where(same & (keys <= queries), 1.0, 0.0)

def masked_scores(mask_ref, k_c, q_pair, qb, span):
    s = dot(k_c, q_pair, 1, 1)
    m = mask_ref[qb, :span]
    return jnp.where(jnp.concatenate([m, m], axis=1) > 0, s, neg_large)

def piece_copies(me_ref, spots, pieces, whole_ref, sems, inward):
    copies = []
    for ref, (offsets, first) in zip(pieces, spots):
        if offsets is None:
            sides = [(ref, whole_ref)]
        else:
            share, cols = ref.shape[1:]
            sides = []
            for i, offset in enumerate(offsets):
                row = pl.multiple_of((me_ref[0] ^ offset) * share, share)
                sides.append((ref.at[i], whole_ref.at[pl.ds(row, share), first : first + cols]))
        for part, place in sides:
            source, target = (part, place) if inward else (place, part)
            copies.append(pltpu.make_async_copy(source, target, sems.at[len(copies)]))
    return copies


def spot_columns(spots):
    return [first if offsets else -1 for offsets, first in spots for _ in (offsets or [None])]


def piece_count(spots):
    return sum(1 if offsets is None else len(offsets) for offsets, _ in spots)


def forward_kernel(spots, me_ref, x_ref, routes_ref, seg_col_ref, seg_row_ref, cos_ref, sin_ref, *refs):
    pieces, refs = refs[: len(spots)], refs[len(spots) :]
    lse_ref, h2_ref, *outs = refs[:9]
    mask_ref, w_ref, h1_ref, q_ref, k_ref, v_ref, o_ref, r1_ref, sems, out_sems = refs[9:]

    def leave(i, source):
        copy = pltpu.make_async_copy(source, outs[i], out_sems.at[i])
        copy.start()
        return copy

    copies = piece_copies(me_ref, spots, pieces, w_ref, sems, True)
    for copy in copies:
        copy.start()
    fill_mask(mask_ref, seg_col_ref, seg_row_ref, x_ref.shape[0])
    for copy in copies:
        copy.wait()
    leaving = [leave(0, w_ref)]
    rows, width = x_ref.shape
    x = x_ref[...].astype(F32)
    gains = w_ref[:, 3072:3200].astype(F32).T
    h1_ref[...] = (x * rms_scale(x) * gains[16:17]).astype(BF)
    leaving.append(leave(1, h1_ref))

    @pl.loop(0, 4)
    def _(j):
        qs = pl.ds(pl.multiple_of(j * 256, 256), 256)
        ks = pl.ds(pl.multiple_of(j * 128, 128), 128)
        vs = pl.ds(pl.multiple_of(1536 + j * 128, 128), 128)
        kw = pl.ds(pl.multiple_of(1024 + j * 128, 128), 128)
        h1 = h1_ref[...]
        cos, sin = cos_ref[...], sin_ref[...]
        q2 = dot(h1, w_ref[:, qs], 1, 0)
        qa, qb_ = crossed(q2[:, :128], q2[:, 128:])
        qa = (qa * cos + swap_halves(qa) * sin).astype(BF) * BF(0.125)
        qb_ = (qb_ * cos + swap_halves(qb_) * sin).astype(BF) * BF(0.125)
        k = dot(h1, w_ref[:, kw], 1, 0)
        k = (k * cos + swap_halves(k) * sin).astype(BF)
        v32 = dot(h1, w_ref[:, vs], 1, 0)
        v = v32.astype(BF)
        q_ref[:, qs] = jnp.concatenate([qa, qb_], axis=1)
        k_ref[:, ks] = k
        v_ref[:, ks] = v
        vt = v32.T.astype(BF)
        lane = lax.broadcasted_iota(jnp.int32, (rows, 128), 1)
        sub = lax.broadcasted_iota(jnp.int32, (128, rows), 0)
        outs = []
        for qb in range(rows // BLOCK):
            low, high = key_range(rows, qb)
            blk = slice(qb * BLOCK, (qb + 1) * BLOCK)
            q_pair = jnp.concatenate([qa[blk], qb_[blk]], axis=0)
            total = None
            for c in range(2):
                k_c = jnp.where(lane[low:high] // 64 == c, k[low:high], BF(0))
                vt_c = jnp.where(sub[:, low:high] // 64 == c, vt[:, low:high], BF(0))
                s = masked_scores(mask_ref, k_c, q_pair, qb, high - low)
                top = jnp.max(s, axis=0, keepdims=True)
                e = jnp.exp(s - top)
                norm = jnp.sum(e, axis=0, keepdims=True)
                p = (e * (1.0 / norm)).astype(BF)
                part = dot(vt_c, p, 1, 0)
                total = part if total is None else total + part
                lse = top + jnp.log(norm)
                lse_ref[j, c : c + 1, blk] = lse[:, :128]
                lse_ref[j, 2 + c : 3 + c, blk] = lse[:, 128:]
            outs.append(total)
        a = jnp.concatenate([t[:, :128] for t in outs], axis=1).T
        b = jnp.concatenate([t[:, 128:] for t in outs], axis=1).T
        o_ref[:, qs] = jnp.concatenate(crossed(a, b), axis=1).astype(BF)

    leaving += [leave(i, ref) for i, ref in ((2, q_ref), (3, k_ref), (4, v_ref), (5, o_ref))]
    r1 = x_ref[...].astype(F32) + dot(o_ref[...], w_ref[:, 2048:3072], 1, 1)
    r1_ref[...] = r1
    leaving.append(leave(6, r1_ref))
    h2 = (r1 * rms_scale(r1) * gains[17:18]).astype(BF)
    h2_ref[:rows] = h2
    logits = dot(h2, w_ref[:, 3072:3200], 1, 0).T[:EXPERTS]
    at = lax.broadcasted_iota(jnp.int32, (EXPERTS, rows), 0)
    chosen = at < 0
    for t in range(routes_ref.shape[0]):
        chosen = chosen | (at == routes_ref[t : t + 1])
    logits = jnp.where(chosen, logits, neg_large)
    ex = jnp.where(chosen, jnp.exp(logits - jnp.max(logits, axis=0, keepdims=True)), 0.0)
    gates = ex / jnp.sum(ex, axis=0, keepdims=True)
    high = gates.astype(BF)
    low = (gates - high.astype(F32)).astype(BF)
    h2_ref[rows:] = jnp.concatenate([high, low], axis=1)
    for copy in leaving:
        copy.wait()

def forward_call(me, x, routes, seg_col, seg_row, cos, sin, pieces, spots):
    rows, width = x.shape
    s = jax.ShapeDtypeStruct
    vmem, anywhere = pl.BlockSpec(memory_space=pltpu.VMEM), pl.BlockSpec(memory_space=pl.ANY)
    return pl.pallas_call(
        functools.partial(forward_kernel, spots),
        in_specs=[pl.BlockSpec(memory_space=pltpu.SMEM)] + [vmem] * 6 + [anywhere] * len(pieces),
        out_specs=[vmem] * 2 + [anywhere] * 7,
        out_shape=[
            s((4, 4, rows), F32),
            s((rows + EXPERTS, width), BF),
            s((width, 3200), BF),
            s((rows, width), BF),
            s((rows, 1024), BF),
            s((rows, 512), BF),
            s((rows, 512), BF),
            s((rows, 1024), BF),
            s((rows, width), F32),
        ],
        scratch_shapes=[
            pltpu.VMEM((rows // BLOCK, BLOCK + MOST_DOC, BLOCK), F32),
            pltpu.VMEM((width, 3200), BF),
            pltpu.VMEM((rows, width), BF),
            pltpu.VMEM((rows, 1024), BF),
            pltpu.VMEM((rows, 512), BF),
            pltpu.VMEM((rows, 512), BF),
            pltpu.VMEM((rows, 1024), BF),
            pltpu.VMEM((rows, width), F32),
            pltpu.SemaphoreType.DMA((piece_count(spots),)),
            pltpu.SemaphoreType.DMA((7,)),
        ],
        cost_estimate=SMALL,
        compiler_params=pltpu.CompilerParams(vmem_limit_bytes=VMEM_ROOM),
    )(me, x, routes, seg_col, seg_row, cos, sin, *pieces)


ARRIVING = 14


def backward_kernel(spots, me_ref, *refs):
    given, refs = refs[:ARRIVING], refs[ARRIVING:]
    lse_ref, seg_col_ref, seg_row_ref, cos_ref, sin_ref, ig_ref = refs[:6]
    pieces, refs = refs[6 : 6 + len(spots)], refs[6 + len(spots) :]
    held, refs = refs[:ARRIVING], refs[ARRIVING:]
    mask_ref, do_ref, dqkv_ref, dr1_ref, wg_ref, sems, in_sems = refs
    p0, p1, p2, p3, r1_ref, cot_ref, h2_ref, w_ref, o_ref, q_ref, k_ref, v_ref, h1_ref, x_ref = held
    parts = [(given[i], held[i]) for i in range(7)]
    for cols in (slice(3072, 3200), slice(2048, 3072), slice(0, 2048)):
        parts.append((given[7].at[:, cols], w_ref.at[:, cols]))
        if cols.start == 2048:
            parts += [(given[i], held[i]) for i in range(8, 12)]
    parts += [(given[12], h1_ref), (given[13], x_ref)]
    copies = [pltpu.make_async_copy(source, target, in_sems.at[i]) for i, (source, target) in enumerate(parts)]
    for copy in copies:
        copy.start()
    fill_mask(mask_ref, seg_col_ref, seg_row_ref, r1_ref.shape[0])
    for copy in copies[:8]:
        copy.wait()
    rows, width = x_ref.shape
    misc = w_ref[:, 3072:3200]
    gains = misc.astype(F32).T

    def up(ref, sl):
        return ref[sl].astype(F32)

    top, tail = slice(0, rows), slice(rows, rows + EXPERTS)
    dh2 = up(p0, top) + up(p1, top) + up(p2, top) + up(p3, top)
    dg = up(p0, tail) + up(p1, tail) + up(p2, tail) + up(p3, tail)
    dg = dg[:, :rows] + dg[:, rows:]
    gates = up(h2_ref, tail)
    gates = gates[:, :rows] + gates[:, rows:]
    h2 = h2_ref[:rows]
    dlog = gates * (dg - jnp.sum(gates * dg, axis=0, keepdims=True))
    dlog = jnp.concatenate([dlog, jnp.zeros((128 - EXPERTS, rows), F32)], axis=0).T.astype(BF)
    dh2 = dh2 + dot(dlog, misc, 1, 1)
    r1 = r1_ref[...]
    s2 = rms_scale(r1)
    w2 = dh2 * gains[17:18]
    gain2_grad = jnp.sum(dh2 * r1 * s2, axis=0, keepdims=True)
    dr1 = cot_ref[...].astype(F32) + s2 * w2 - r1 * (s2 * s2 * s2) * jnp.mean(w2 * r1, axis=-1, keepdims=True)
    dr1_ref[...] = dr1
    dz = dr1.astype(BF)
    for copy in copies[8:13]:
        copy.wait()
    wg_ref[:, 2048:3072] = dot(dz, o_ref[...], 0, 0).astype(BF)
    do_ref[...] = dot(dz, w_ref[:, 2048:3072], 1, 0).astype(BF)
    router_t = dot(dlog, h2, 0, 0)

    @pl.loop(0, 4)
    def _(j):
        qs = pl.ds(pl.multiple_of(j * 256, 256), 256)
        ks = pl.ds(pl.multiple_of(j * 128, 128), 128)
        vs = pl.ds(pl.multiple_of(1536 + j * 128, 128), 128)
        kw = pl.ds(pl.multiple_of(1024 + j * 128, 128), 128)
        cos, sin = cos_ref[...], sin_ref[...]
        def back(g):
            return g * cos - swap_halves(g) * sin
        q, k, v = q_ref[:, qs], k_ref[:, ks], v_ref[:, ks]
        do = do_ref[:, qs].astype(F32)
        do = jnp.concatenate(crossed(do[:, :128], do[:, 128:]), axis=1).astype(BF)
        kt = k.astype(F32).T.astype(BF)
        lane = lax.broadcasted_iota(jnp.int32, (rows, 128), 1)
        sub = lax.broadcasted_iota(jnp.int32, (128, rows), 0)
        dks = [jnp.zeros((BLOCK, 128), F32) for _ in range(rows // BLOCK)]
        dvs = [jnp.zeros((BLOCK, 128), F32) for _ in range(rows // BLOCK)]
        dqs = []
        for qb in range(rows // BLOCK):
            low, high = key_range(rows, qb)
            blk = slice(qb * BLOCK, (qb + 1) * BLOCK)
            q_pair = jnp.concatenate([q[blk, :128], q[blk, 128:]], axis=0)
            do_pair = jnp.concatenate([do[blk, :128], do[blk, 128:]], axis=0)
            dq_t = None
            for c in range(2):
                mine = lane[low:high] // 64 == c
                k_c = jnp.where(mine, k[low:high], BF(0))
                v_c = jnp.where(mine, v[low:high], BF(0))
                kt_c = jnp.where(sub[:, low:high] // 64 == c, kt[:, low:high], BF(0))
                s = masked_scores(mask_ref, k_c, q_pair, qb, high - low)
                lse = jnp.concatenate([lse_ref[j, c : c + 1, blk], lse_ref[j, 2 + c : 3 + c, blk]], axis=1)
                p = jnp.exp(s - lse)
                dp = dot(v_c, do_pair, 1, 1)
                inner = jnp.sum(p * dp, axis=0, keepdims=True)
                ds = (p * (dp - inner)).astype(BF)
                dk = dot(ds, q_pair, 1, 0)
                dv = dot(p.astype(BF), do_pair, 1, 0)
                t = dot(kt_c, ds, 1, 0)
                dq_t = t if dq_t is None else dq_t + t
                for i, kb in enumerate(range(low // BLOCK, high // BLOCK)):
                    sl = slice(i * BLOCK, (i + 1) * BLOCK)
                    dks[kb] = dks[kb] + jnp.where(mine[sl], dk[sl], 0.0)
                    dvs[kb] = dvs[kb] + jnp.where(mine[sl], dv[sl], 0.0)
            dqs.append(dq_t)
        dqa = jnp.concatenate([t[:, :128] for t in dqs], axis=1).T * 0.125
        dqb = jnp.concatenate([t[:, 128:] for t in dqs], axis=1).T * 0.125
        dqkv_ref[:, qs] = jnp.concatenate(crossed(back(dqa), back(dqb)), axis=1).astype(BF)
        dqkv_ref[:, kw] = back(jnp.concatenate(dks, axis=0)).astype(BF)
        dqkv_ref[:, vs] = jnp.concatenate(dvs, axis=0).astype(BF)

    for copy in copies[13:]:
        copy.wait()
    leaving = piece_copies(me_ref, spots, pieces, wg_ref, sems, False)
    wg_ref[:, :1536] = dot(h1_ref[...], dqkv_ref[:, :1536], 0, 0).astype(BF)
    early = [i for i, first in enumerate(spot_columns(spots)) if first == 0]
    for i in early:
        leaving[i].start()
    wg_ref[:, 1536:2048] = dot(h1_ref[...], dqkv_ref[:, 1536:], 0, 0).astype(BF)
    dh1 = dot(dqkv_ref[...], w_ref[:, :2048], 1, 1)
    x = x_ref[...].astype(F32)
    s1 = rms_scale(x)
    w1 = dh1 * gains[16:17]
    gain1_grad = jnp.sum(dh1 * x * s1, axis=0, keepdims=True)
    at = lax.broadcasted_iota(jnp.int32, (128, width), 0)
    misc_t = jnp.where(at == 16, gain1_grad, jnp.where(at == 17, gain2_grad, router_t))
    wg_ref[:, 3072:3200] = misc_t.T.astype(BF)
    for i in range(len(leaving)):
        if i not in early:
            leaving[i].start()
    ig_ref[...] = dr1_ref[...] + s1 * w1 - x * (s1 * s1 * s1) * jnp.mean(w1 * x, axis=-1, keepdims=True)
    for copy in leaving:
        copy.wait()


def backward_call(me, parts, x, r1, cot, h1, h2, w, q, k, v, o, lse, seg_col, seg_row, cos, sin, piece_shapes, spots):
    rows, width = x.shape
    s = jax.ShapeDtypeStruct
    vmem, anywhere = pl.BlockSpec(memory_space=pltpu.VMEM), pl.BlockSpec(memory_space=pl.ANY)
    arriving = [*parts, r1, cot, h2, w, o, q, k, v, h1, x]
    return pl.pallas_call(
        functools.partial(backward_kernel, spots),
        in_specs=[pl.BlockSpec(memory_space=pltpu.SMEM)] + [anywhere] * ARRIVING + [vmem] * 5,
        out_specs=[vmem] + [anywhere] * len(spots),
        out_shape=[s((rows, width), F32)] + [s(shape, BF) for shape in piece_shapes],
        scratch_shapes=[pltpu.VMEM(a.shape, a.dtype) for a in arriving]
        + [
            pltpu.VMEM((rows // BLOCK, BLOCK + MOST_DOC, BLOCK), F32),
            pltpu.VMEM((rows, 1024), BF),
            pltpu.VMEM((rows, 2048), BF),
            pltpu.VMEM((rows, width), F32),
            pltpu.VMEM((width, 3200), BF),
            pltpu.SemaphoreType.DMA((piece_count(spots),)),
            pltpu.SemaphoreType.DMA((ARRIVING + 2,)),
        ],
        cost_estimate=SMALL,
        compiler_params=pltpu.CompilerParams(vmem_limit_bytes=VMEM_ROOM),
    )(me, *arriving, lse, seg_col, seg_row, cos, sin)


def expert_kernel(plan, count, place_ref, *refs):
    blocks = len(plan)
    arrays, refs = refs[:count], refs[count:]
    w_refs = refs[:6]
    ug0, ug1, da0, da1, db0, db1, h_all, g_all = refs[6:14]
    backs, forths = refs[14 : 14 + blocks], refs[14 + blocks : 14 + 2 * blocks]
    h_buf, g_buf, back_buf, forth_buf, gates_buf, dg_buf, sems, out_sems = refs[14 + 2 * blocks :]
    rows = g_buf.shape[1]
    step = pl.program_id(0)
    slot = lax.rem(step, 2)

    def copies(i):
        found = []
        for buf, parts in ((h_buf, plan[i][0]), (g_buf, plan[i][1])):
            for array, start, size, at in parts:
                sem = sems.at[i % 2, len(found)]
                found.append(
                    pltpu.make_async_copy(
                        arrays[array].at[pl.ds(start, size)], buf.at[i % 2, pl.ds(at, size)], sem
                    )
                )
        return found

    def results(i):
        return (
            pltpu.make_async_copy(back_buf.at[i % 2], backs[i], out_sems.at[i % 2, 0]),
            pltpu.make_async_copy(forth_buf.at[i % 2], forths[i], out_sems.at[i % 2, 1]),
        )

    for i in range(blocks):

        @pl.when(step == i)
        def _(i=i):
            if i == 0:
                for copy in copies(0):
                    copy.start()
            if i + 1 < blocks:
                for copy in copies(i + 1):
                    copy.start()
            if i >= 2:
                for copy in results(i - 2):
                    copy.wait()
            for copy in copies(i):
                copy.wait()

    tail = h_buf[slot, rows:].astype(F32)
    tail = tail[:, :rows] + tail[:, rows:]
    gates_buf[...] = jnp.concatenate([tail, jnp.zeros((128 - EXPERTS, rows), F32)], axis=0).T
    place = place_ref[0]
    tile = rows // 2
    lane = lax.broadcasted_iota(jnp.int32, (tile, 128), 1)

    @pl.loop(0, 2)
    def _(r):
        part = pl.ds(pl.multiple_of(r * tile, tile), tile)
        h, g, gates = h_buf[slot, part], g_buf[slot, part], gates_buf[part]
        h_all[part], g_all[part] = h, g
        totals = []
        for e, (ug_ref, da_ref, db_ref) in enumerate(((ug0, da0, db0), (ug1, da1, db1))):
            wg_ref, wu_ref, wd_ref = w_refs[3 * e : 3 * e + 3]
            ff = wg_ref.shape[2]
            gate = jnp.sum(jnp.where(lane == place * MINE + e, gates, 0.0), axis=1, keepdims=True)
            total = 0.0
            for half in range(2):
                sl = slice(half * ff // 2, (half + 1) * ff // 2)
                a = dot(h, wg_ref[0, :, sl], 1, 0)
                b = dot(h, wu_ref[0, :, sl], 1, 0)
                gd = dot(g, wd_ref[0, :, sl], 1, 0)
                sigma = 0.5 * jnp.tanh(0.5 * a) + 0.5
                silu = a * sigma
                u = (silu * b).astype(BF).astype(F32)
                total = total + jnp.sum(u * gd, axis=1, keepdims=True)
                ug_ref[part, sl] = (u * gate).astype(BF)
                du = gd * gate
                db_ref[part, sl] = (du * silu).astype(BF)
                da_ref[part, sl] = (du * b * (sigma * (1.0 + a * (1.0 - sigma)))).astype(BF)
            totals.append(total)
        back = dot(da0[part], w_refs[0][0], 1, 1) + dot(db0[part], w_refs[1][0], 1, 1)
        back = back + dot(da1[part], w_refs[3][0], 1, 1) + dot(db1[part], w_refs[4][0], 1, 1)
        back_buf[slot, part] = back.astype(BF)
        forth = dot(ug0[part], w_refs[2][0], 1, 1) + dot(ug1[part], w_refs[5][0], 1, 1)
        forth_buf[slot, part] = forth.astype(BF)
        dg_buf[part] = jnp.where(lane == 0, totals[0], totals[1])

    dg = dg_buf[...].T
    at = lax.broadcasted_iota(jnp.int32, (EXPERTS, rows), 0)
    dg = jnp.where(at == place * MINE, dg[0:1], jnp.where(at == place * MINE + 1, dg[1:2], 0.0))
    high = dg.astype(BF)
    low = (dg - high.astype(F32)).astype(BF)
    back_buf[slot, rows:] = jnp.concatenate([high, low], axis=1)

    for i in range(blocks):

        @pl.when(step == i)
        def _(i=i):
            for copy in results(i):
                copy.start()
            if i == blocks - 1:
                for copy in (*results(i - 1), *results(i)):
                    copy.wait()


def expert_call(place, arrays, plan, weights):
    _, width, ff = weights.shape
    blocks = len(plan)
    rows = sum(piece[2] for piece in plan[0][1])
    most = max(len(h) + len(g) for h, g in plan)
    s = jax.ShapeDtypeStruct
    at = lambda i: (i, 0)
    anywhere = pl.BlockSpec(memory_space=pl.ANY)
    hidden, tile = pl.BlockSpec((rows, ff), at), pl.BlockSpec((rows, width), at)
    out = pl.pallas_call(
        functools.partial(expert_kernel, plan, len(arrays)),
        grid=(blocks,),
        in_specs=[pl.BlockSpec(memory_space=pltpu.SMEM)]
        + [anywhere] * len(arrays)
        + [pl.BlockSpec((1, width, ff), lambda i, k=k: (k, 0, 0), pipeline_mode=pl.Buffered(1)) for k in range(6)],
        out_specs=[hidden] * 6 + [tile] * 2 + [anywhere] * (2 * blocks),
        out_shape=[s((PLANE * rows, ff), BF)] * 6
        + [s((PLANE * rows, width), BF)] * 2
        + [s((rows + EXPERTS, width), BF)] * blocks
        + [s((rows, width), BF)] * blocks,
        scratch_shapes=[
            pltpu.VMEM((2, rows + EXPERTS, width), BF),
            pltpu.VMEM((2, rows, width), BF),
            pltpu.VMEM((2, rows + EXPERTS, width), BF),
            pltpu.VMEM((2, rows, width), BF),
            pltpu.VMEM((rows, 128), F32),
            pltpu.VMEM((rows, 128), F32),
            pltpu.SemaphoreType.DMA((2, most)),
            pltpu.SemaphoreType.DMA((2, 2)),
        ],
        cost_estimate=SMALL,
        compiler_params=pltpu.CompilerParams(vmem_limit_bytes=44 * MIB),
    )(place, *arrays, *[weights] * 6)
    return out[:8], out[8 : 8 + blocks], out[8 + blocks :]


STEPS = 4


def weight_grad_kernel(count, sums, sum_steps, left_ref, *refs):
    rights, refs = refs[:count], refs[count:]
    terms, refs = refs[: 2 * sums], refs[2 * sums :]
    out_ref, totals, acc_ref = refs[0], refs[1:-1], refs[-1]
    k = pl.program_id(0)
    ff = rights[0].shape[1]
    part = dot(left_ref[...], jnp.concatenate([r[...] for r in rights], axis=1), 0, 0)

    @pl.when(k < sum_steps)
    def _():
        for i in range(sums):
            totals[i][...] = (terms[2 * i][...].astype(F32) + terms[2 * i + 1][...].astype(F32)).astype(BF)

    @pl.when(k == 0)
    def _():
        acc_ref[...] = part

    @pl.when(k > 0)
    def _():
        acc_ref[...] += part

    @pl.when(k == STEPS - 1)
    def _():
        for t in range(count):
            out_ref[t] = acc_ref[:, t * ff : (t + 1) * ff].astype(BF)


def weight_grads(left, rights, pairs=()):
    total, width = left.shape
    ff = rights[0].shape[1]
    count = len(rights)
    step = total // STEPS
    row = lambda i: (i, 0)
    rows = pairs[0][0].shape[0] if pairs else 0
    sum_steps = next(n for n in (4, 3, 2, 1) if rows % (16 * n) == 0)
    tile = pl.BlockSpec((rows // sum_steps, width), lambda i: (jnp.minimum(i, sum_steps - 1), 0))
    s = jax.ShapeDtypeStruct
    out = pl.pallas_call(
        functools.partial(weight_grad_kernel, count, len(pairs), sum_steps),
        grid=(STEPS,),
        in_specs=[pl.BlockSpec((step, width), row)]
        + [pl.BlockSpec((step, ff), row)] * count
        + [tile] * (2 * len(pairs)),
        out_specs=[pl.BlockSpec((count, width, ff), lambda i: (0, 0, 0), pipeline_mode=pl.Buffered(1))]
        + [tile] * len(pairs),
        out_shape=[s((count, width, ff), BF)] + [s((rows, width), BF)] * len(pairs),
        scratch_shapes=[pltpu.VMEM((width, count * ff), F32)],
        cost_estimate=SMALL,
        compiler_params=pltpu.CompilerParams(vmem_limit_bytes=VMEM_ROOM),
    )(left, *rights, *[term for pair in pairs for term in pair])
    return out[0], out[1:]


def up(v):
    return v.astype(F32)


def after(value, *others):
    return lax.optimization_barrier((value, *others))[0]


CUT = 1536
COLUMNS = 3200


def make_local(n):
    outer = n // PLANE
    plane_groups = [[PLANE * z + i for i in range(PLANE)] for z in range(outer)]
    outer_groups = [[PLANE * z + i for z in range(outer)] for i in range(PLANE)]
    pieced = outer == 4

    def swap(array, offset):
        return lax.ppermute(array, "dp", [(i, i ^ offset) for i in range(n)])

    along_z = [PLANE * k for k in range(4)]

    def dense_gather(part, *earlier):
        if not pieced:
            return [lax.all_gather(part, "dp", axis=0, tiled=True)], [(None, 0)]
        line = after([part] + [swap(part, k) for k in along_z[1:]], *earlier)
        left, right = jnp.stack([t[:, :CUT] for t in line]), jnp.stack([t[:, CUT:] for t in line])
        left_x, right_y = swap(left, 2), swap(right, 4)
        left_y, right_x = swap(left, 4), swap(right, 2)
        left_xy, right_xy = swap(left_x, 4), swap(right_y, 2)
        found = [(left, 0, 0), (left_x, 2, 0), (left_y, 4, 0), (left_xy, 6, 0)]
        found += [(right, 0, CUT), (right_x, 2, CUT), (right_y, 4, CUT), (right_xy, 6, CUT)]
        found += [(swap(piece, 1), offset + 1, first) for piece, offset, first in found]
        return [f[0] for f in found], [([f[1] + k for k in along_z], f[2]) for f in found]

    def grad_spots(share):
        if not pieced:
            return [(n * share, COLUMNS)], [(None, 0)]
        shapes, spots = [], []
        for core in (1, 0):
            for major, minor, first, cols in ((2, 4, 0, CUT), (4, 2, CUT, COLUMNS - CUT)):
                for far in (0, major):
                    shapes.append((8, share, cols))
                    spots.append(([core + far + d + k for d in (0, minor) for k in along_z], first))
        return shapes, spots

    def dense_sum(pieces, earlier):
        if not pieced:
            return up(lax.psum_scatter(pieces[0], "dp", scatter_dimension=0, tiled=True))

        def add(a, b):
            return (up(a) + up(b)).astype(BF)

        near_l, far_l, near_r, far_r = (add(keep, swap(sent, 1)) for sent, keep in zip(pieces[:4], pieces[4:]))
        far_l, far_r = after((far_l, far_r), earlier)
        got_l, got_r = swap(far_l, 2), swap(far_r, 4)
        sent_l, sent_r = add(near_l[4:], got_l[4:]), add(near_r[4:], got_r[4:])
        left = add(add(near_l[:4], got_l[:4]), swap(sent_l, 4))
        right = add(add(near_r[:4], got_r[:4]), swap(sent_r, 2))
        both = jnp.concatenate([left, right], axis=2)
        total = up(both[0])
        for k in range(1, 4):
            total = total + up(swap(both[k], PLANE * k))
        return total

    def both_cores(same_core):
        return [b for part in same_core for b in (part, swap(part, 1))]

    def local(
        tokens,
        query_weight,
        key_projection_weight,
        value_projection_weight,
        output_weight,
        first_gain,
        second_gain,
        router_weight,
        gate_weight,
        up_weight,
        down_weight,
        routes,
        segments,
        cotangent,
    ):
        rows, width = tokens.shape
        ff = gate_weight.shape[2]
        share = query_weight.shape[0]
        me = lax.axis_index("dp").astype(jnp.int32).reshape(1)
        place = lax.rem(me, PLANE)

        expert_part = jnp.stack(
            [w.reshape(PLANE, MINE, share, ff) for w in (gate_weight, up_weight, down_weight.transpose(0, 2, 1))],
            axis=2,
        )
        dense_part = jnp.concatenate(
            [
                query_weight,
                key_projection_weight,
                value_projection_weight,
                output_weight.T,
                router_weight,
                first_gain[:, None],
                second_gain[:, None],
                jnp.zeros((share, 128 - EXPERTS - 2), BF),
            ],
            axis=1,
        )
        dense_part = after(dense_part, expert_part)
        expert_part = lax.all_to_all(
            expert_part, "dp", split_axis=0, concat_axis=0, axis_index_groups=plane_groups
        )

        expert_part = expert_part.transpose(1, 2, 0, 3, 4).reshape(3 * MINE, PLANE * share, ff)
        weights = lax.all_gather(expert_part, "dp", axis=1, tiled=True, axis_index_groups=outer_groups)

        positions = jnp.arange(rows, dtype=F32)
        frequency = 10000.0 ** (-2.0 * jnp.arange(HEAD_SIZE // 2, dtype=F32) / HEAD_SIZE)
        angles = positions[:, None] * frequency[None, :]
        cosine, sine = jnp.cos(angles), jnp.sin(angles)
        cosine = jnp.concatenate([cosine] * 4, axis=1)
        sine = jnp.concatenate([-sine, sine, -sine, sine], axis=1)
        seg_col = segments.reshape(rows, 1)
        seg_row = segments.reshape(1, rows)

        half = rows // 2
        pieces, spots = dense_gather(dense_part, cosine, sine, seg_col, expert_part)
        late = after(cotangent, *pieces)
        cot_x, cot_y = swap(late, 2), swap(late, 4)

        lse, h2, dense, h1, q, k, v, o, r1 = forward_call(
            me, tokens, routes.T, seg_col, seg_row, cosine, sine, pieces, spots
        )
        h2 = after(h2, cot_x, cot_y)
        h2_x, h2_y, h2_core = swap(h2, 2), swap(h2, 4), swap(h2, 1)
        cot_core = swap(cotangent, 1)
        h2_x, h2_y, cot_x, cot_y = after((h2_x, h2_y, cot_x, cot_y), h2_core, cot_core)
        corner_x = swap(jnp.concatenate([h2_y[:half], cot_y[:half]], axis=0), 2)
        corner_y = swap(jnp.concatenate([h2_x[half:], cot_x[half:]], axis=0), 4)
        cores = [swap(t, 1) for t in (h2_x, cot_x, h2_y, cot_y)]
        corner_x, corner_y = after((corner_x, corner_y), *cores)
        long = rows + EXPERTS

        def pieces_of(h, g):
            return ([(h, 0, long, 0)], [(g, 0, rows, 0)])

        first_arrays = [corner_x, swap(corner_x, 1), corner_y, swap(corner_y, 1), h2_x, cores[0], cot_x, cores[1]]
        first_plan = [
            (
                [(i, 0, half, 0), (i + 2, 0, long - half, half)],
                [(i, half, half, 0), (i + 2, long - half, half, half)],
            )
            for i in range(2)
        ]
        first_plan += [pieces_of(i, 2 + i) for i in (4, 5)]
        second_arrays = [h2, h2_core, h2_y, cores[2], cotangent, cot_core, cot_y, cores[3]]
        second_plan = [pieces_of(8 + i, 12 + i) for i in range(4)]

        def outer_sum(grads):
            return lax.psum_scatter(grads, "dp", scatter_dimension=1, tiled=True, axis_index_groups=outer_groups)

        def with_core(block, other):
            return (up(block) + up(other)).astype(BF)

        def together(*values):
            return lax.optimization_barrier(values)

        top, low = slice(0, half), slice(half, None)

        kept, back, out = expert_call(place, first_arrays + second_arrays, first_plan + second_plan, weights)
        core_xy, core_x, core_y = swap(back[1], 1), swap(back[3], 1), swap(back[7], 1)
        sum_xy = [with_core(back[0][part], core_xy[part]) for part in (top, low)]
        sum_xy, core_x, core_y, kept, back, out = together(sum_xy, core_x, core_y, kept, back, out)

        ug0, ug1, da0, da1, db0, db1, tokens_all, grads_all = kept
        grads_d, (sum_x, sum_y) = weight_grads(grads_all, [ug0, ug1], [(back[2], core_x), (back[6], core_y)])
        via_x, via_y, out_core = swap(sum_xy[0], 2), swap(sum_xy[1], 4), [swap(out[i], 1) for i in (1, 3, 7)]
        grads_d, sum_x, sum_y, via_x, via_y, out_core, kept, out, back = together(
            grads_d, sum_x, sum_y, via_x, via_y, out_core, kept, out, back
        )
        sums_d = outer_sum(grads_d)
        sum_y = with_core(sum_y, jnp.pad(via_x, ((0, sum_y.shape[0] - half), (0, 0))))
        sum_x = with_core(sum_x, jnp.pad(via_y, ((half, 0), (0, 0))))
        sum_x, sum_y, kept, back, out, out_core = together(sum_x, sum_y, kept, back, out, out_core)

        _, _, da0, da1, db0, db1, tokens_all, _ = kept
        grads_gu, (out_xy, out_x, out_y) = weight_grads(
            tokens_all,
            [da0, da1, db0, db1],
            [(out[0], out_core[0]), (out[2], out_core[1]), (out[6], out_core[2])],
        )
        got_x, got_y, core_own, out_core_own = swap(sum_x, 2), swap(sum_y, 4), swap(back[5], 1), swap(out[5], 1)
        grads_gu, got_x, got_y, core_own, out_core_own, out_xy, out_x, out_y, _ = together(
            grads_gu, got_x, got_y, core_own, out_core_own, out_xy, out_x, out_y, (first_arrays, second_arrays)
        )
        sums_gu = outer_sum(grads_gu)
        got = [back[4], core_own, got_x, got_y]
        got, out_x, out_y, out_xy = together(got, out_x, out_y, [out_xy[top], out_xy[low]])

        shapes, grad_places = grad_spots(share)
        input_grad, *grad_pieces = backward_call(
            me, got, tokens, r1, cotangent, h1, h2, dense, q, k, v, o, lse, seg_col, seg_row, cosine, sine,
            shapes, grad_places,
        )
        got_out = [swap(out_x, 2), swap(out_y, 4), swap(out_xy[0], 6)]
        input_grad, grad_pieces, got_out, out_xy = together(input_grad, grad_pieces, got_out, out_xy)
        got_out_low = swap(out_xy[1], 6)
        output = r1 + up(out[4]) + up(out_core_own) + up(got_out[0]) + up(got_out[1])
        output_top, output_low = (output[top] + up(got_out[2])).astype(BF), output[low]
        owned = jnp.concatenate([sums_d, sums_gu], axis=0).reshape(3 * MINE, PLANE, share, ff).transpose(1, 0, 2, 3)
        dense_grads = dense_sum(grad_pieces, (got_out_low, output_top, output_low))
        output = jnp.concatenate([output_top, (output_low + up(got_out_low)).astype(BF)], axis=0)
        owned = lax.all_to_all(owned, "dp", split_axis=0, concat_axis=0, axis_index_groups=plane_groups)

        def experts_of(kind):
            return up(owned[:, MINE * kind : MINE * (kind + 1)]).reshape(EXPERTS, share, ff)

        down_out, gate_out, up_out = experts_of(0).transpose(0, 2, 1), experts_of(1), experts_of(2)
        return (
            output,
            input_grad,
            dense_grads[:, :1024],
            dense_grads[:, 1024:1536],
            dense_grads[:, 1536:2048],
            dense_grads[:, 2048:3072].T,
            dense_grads[:, 3072 + EXPERTS],
            dense_grads[:, 3073 + EXPERTS],
            dense_grads[:, 3072 : 3072 + EXPERTS],
            gate_out,
            up_out,
            down_out,
        )

    return local


def solution(mesh):
    row, col, one = P("dp", None), P(None, "dp"), P("dp")
    middle, last = P(None, "dp", None), P(None, None, "dp")
    in_specs = (row, row, row, row, col, one, one, row, middle, middle, last, row, row, row)
    out_specs = (row, row, row, row, row, col, one, one, row, middle, middle, last)
    return jax.shard_map(
        make_local(mesh.shape["dp"]), mesh=mesh, in_specs=in_specs, out_specs=out_specs, check_vma=False
    )
```

profile of v0, /device:TPU:0, one launch (start us, length us, event | category | flops | bytes accessed | tf_op | source)
XLA Modules:
  0.0 412.7 jit_solution(9508597312555912811)
XLA Ops:
  7.2 2.7 pad_maximum_fusion
  9.9 5.3 %all-to-all-start = ((bf16[8,2,3,32,512]{4,3,2,1,0:T(8,128)(2,1)}), bf16[8,2,3,32,512]{4,3,2,1,0:T(8,128)(2,1)S(1)}, u32[]{:S(2)}, u32[]{:S(2)}) async-start(bf16[8,2,3,32,512]{4,3,2,1,0:T(8,128)(2,1)} %pad_maximum_fusion), calls=%async_computation | async-start | bytes 3145728 | tf_op jit(solution)/shard_map/all_to_all | solution.py:665
  15.7 1.6 collective-permute-start
  17.3 2.6 collective-permute-start.1
  22.4 13.8 %all-to-all-done = bf16[8,2,3,32,512]{4,3,2,1,0:T(8,128)(2,1)S(1)} async-done(((bf16[8,2,3,32,512]{4,3,2,1,0:T(8,128)(2,1)}), bf16[8,2,3,32,512]{4,3,2,1,0:T(8,128)(2,1)S(1)}, u32[]{:S(2)}, u32[]{:S(2)}) %all-to-all-start) | async-done | bytes 1572896 | tf_op jit(solution)/shard_map/all_to_all | solution.py:665
  39.2 1.4 collective-permute-start.4
  40.6 1.5 collective-permute-start.6
  42.1 8.6 %collective-permute-done.3.refs_1_ = bf16[4,32,1536]{2,1,0:T(8,128)(2,1)S(1)} collective-permute-done((bf16[4,32,1536]{2,1,0:T(8,128)(2,1)S(1)}, bf16[4,32,1536]{2,1,0:T(8,128)(2,1)S(1)}, u32[]{:S(2)}, u32[]{:S(2)}) %collective-permute-start.3) | collective-permute-done | bytes 393248 | tf_op jit(solution)/shard_map/ppermute | solution.py:575
  51.3 4.4 %collective-permute-done.4.refs_2_ = bf16[4,32,1536]{2,1,0:T(8,128)(2,1)S(1)} collective-permute-done((bf16[4,32,1536]{2,1,0:T(8,128)(2,1)S(1)}, bf16[4,32,1536]{2,1,0:T(8,128)(2,1)S(1)}, u32[]{:S(2)}, u32[]{:S(2)}) %collective-permute-start.4) | collective-permute-done | bytes 393248 | tf_op jit(solution)/shard_map/ppermute | solution.py:575
  57.5 2.3 collective-permute-done.6.refs_5_
  60.3 5.9 %collective-permute-done.8.refs_7_ = bf16[4,32,1664]{2,1,0:T(8,128)(2,1)S(1)} collective-permute-done((bf16[4,32,1664]{2,1,0:T(8,128)(2,1)S(1)}, bf16[4,32,1664]{2,1,0:T(8,128)(2,1)S(1)}, u32[]{:S(2)}, u32[]{:S(2)}) %collective-permute-start.8) | collective-permute-done | bytes 426016 | tf_op jit(solution)/shard_map/ppermute | solution.py:575
  66.8 1.7 collective-permute-done.11.refs_10_
  69.2 2.2 collective-permute-start.17
  71.3 1.3 collective-permute-start.18
  73.6 21.5 %shard_map.229 = (f32[4,4,512]{2,1,0:T(4,128)}, bf16[528,1024]{1,0:T(8,128)(2,1)}, bf16[1024,3200]{1,0:T(8,128)(2,1)}, bf16[512,1024]{1,0:T(8,128)(2,1)}, bf16[5...) custom-call(s32[1]{0:T(128)} %bitcast.me_ref, ...), custom_call_target="tpu_custom_call" | custom-call | flops 1 | bytes 1 | tf_op jit(solution)/shard_map/pallas_call | solution.py:179
  96.6 1.3 collective-permute-start.20
  98.4 3.7 collective-permute-done.22.refs_13_
  102.1 19.2 %collective-permute-done.19.refs_4_ = bf16[528,1024]{1,0:T(8,128)(2,1)S(1)} collective-permute-done((bf16[528,1024]{1,0:T(8,128)(2,1)}, bf16[528,1024]{1,0:T(8,128)(2,1)S(1)}, u32[]{:S(2)}, u32[]{:S(2)}) %collective-permute-start.19) | collective-permute-done | bytes 1081376 | tf_op jit(solution)/shard_map/ppermute | solution.py:575
  121.9 1.4 collective-permute-start.23
  123.5 1.4 collective-permute-start.24
  125.4 19.9 %collective-permute-done.23.refs_0_ = bf16[512,1024]{1,0:T(8,128)(2,1)S(1)} collective-permute-done((bf16[512,1024]{1,0:T(8,128)(2,1)S(1)}, bf16[512,1024]{1,0:T(8,128)(2,1)S(1)}, u32[]{:S(2)}, u32[]{:S(2)}) %collective-permute-start.23) | collective-permute-done | bytes 1048608 | tf_op jit(solution)/shard_map/ppermute | solution.py:575
  145.3 2.6 collective-permute-done.28.refs_15_
  148.6 3.7 collective-permute-done.29.refs_1_
  153.3 66.9 %shard_map.230 = (bf16[4096,512]{1,0:T(8,128)(2,1)}, bf16[4096,512]{1,0:T(8,128)(2,1)}, bf16[4096,512]{1,0:T(8,128)(2,1)}, bf16[4096,512]{1,0:T(8,128)(2,1)}, bf...) custom-call(s32[1]{0:T(128)S(6)} %rem.18.place_ref, ...), custom_call_target="tpu_custom_call" | custom-call | flops 1 | bytes 1 | tf_op jit(solution)/shard_map/pallas_call | solution.py:473
  220.9 2.3 collective-permute-done.31
  223.2 2.0 add_convert_fusion.8
  227.1 1.3 collective-permute-start.35
  229.4 16.1 %shard_map.231 = (bf16[2,1024,512]{2,1,0:T(8,128)(2,1)}, bf16[528,1024]{1,0:T(8,128)(2,1)}, bf16[528,1024]{1,0:T(8,128)(2,1)}) custom-call(bf16[4096,1024]{1,0:T(8,128)(2,1)} %get-tuple-element.205.left_ref, bf16[4096,512]{1,0:T(8,128)(2,1)} %get-tuple-element.206.refs_0_, bf16[4096,512]{1,0:T(8,128)(2,1)} %get-tuple-element.207.refs_1_, ...), custom_call_target="tpu_custom_call" | custom-call | flops 1 | bytes 1 | tf_op jit(solution)/shard_map/pallas_call | solution.py:540
  245.6 2.7 add_convert_fusion
  248.3 2.3 add_convert_fusion.1
  252.8 28.2 %shard_map.232 = (bf16[4,1024,512]{2,1,0:T(8,128)(2,1)}, bf16[512,1024]{1,0:T(8,128)(2,1)}, bf16[512,1024]{1,0:T(8,128)(2,1)}, bf16[512,1024]{1,0:T(8,128)(2,1)}) custom-call(bf16[4096,1024]{1,0:T(8,128)(2,1)} %get-tuple-element.252.left_ref, bf16[4096,512]{1,0:T(8,128)(2,1)} %get-tuple-element.253.refs_0_, bf16[4096,512]{1,0:T(8,128)(2,1)} %get-tuple-element.254.refs_1_, ...), custom_call_target="tpu_custom_call" | custom-call | flops 1 | bytes 1 | tf_op jit(solution)/shard_map/pallas_call | solution.py:540
  284.5 1.3 collective-permute-start.44
  287.0 32.6 %shard_map.233 = (f32[512,1024]{1,0:T(8,128)}, bf16[8,32,1536]{2,1,0:T(8,128)(2,1)}, bf16[8,32,1536]{2,1,0:T(8,128)(2,1)}, bf16[8,32,1664]{2,1,0:T(8,128)(2,1)},...) custom-call(s32[1]{0:T(128)} %bitcast.me_ref, ...), custom_call_target="tpu_custom_call" | custom-call | flops 1 | bytes 1 | tf_op jit(solution)/shard_map/pallas_call | solution.py:342
  320.9 1.7 collective-permute-start.46
  323.6 2.8 convert_add_fusion
  326.5 8.3 %collective-permute-done.46 = bf16[256,1024]{1,0:T(8,128)(2,1)S(1)} collective-permute-done((bf16[256,1024]{1,0:T(8,128)(2,1)S(1)}, bf16[256,1024]{1,0:T(8,128)(2,1)S(1)}, u32[]{:S(2)}, u32[]{:S(2)}) %collective-permute-start.46) | collective-permute-done | bytes 524320 | tf_op jit(solution)/shard_map/ppermute | solution.py:575
  334.8 1.4 fusion
  339.9 15.3 %collective-permute-done.50 = bf16[8,32,1536]{2,1,0:T(8,128)(2,1)S(1)} collective-permute-done((bf16[8,32,1536]{2,1,0:T(8,128)(2,1)S(1)}, bf16[8,32,1536]{2,1,0:T(8,128)(2,1)S(1)}, u32[]{:S(2)}, u32[]{:S(2)}) %collective-permute-start.50) | collective-permute-done | bytes 786464 | tf_op jit(solution)/shard_map/ppermute | solution.py:575
  355.8 4.3 %collective-permute-done.53 = bf16[8,32,1664]{2,1,0:T(8,128)(2,1)S(1)} collective-permute-done((bf16[8,32,1664]{2,1,0:T(8,128)(2,1)S(1)}, bf16[8,32,1664]{2,1,0:T(8,128)(2,1)S(1)}, u32[]{:S(2)}, u32[]{:S(2)}) %collective-permute-start.53) | collective-permute-done | bytes 852000 | tf_op jit(solution)/shard_map/ppermute | solution.py:575
  360.8 5.5 %collective-permute-done.51 = bf16[4,32,1536]{2,1,0:T(8,128)(2,1)S(1)} collective-permute-done((bf16[4,32,1536]{2,1,0:T(8,128)(2,1)S(1)}, bf16[4,32,1536]{2,1,0:T(8,128)(2,1)S(1)}, u32[]{:S(2)}, u32[]{:S(2)}) %collective-permute-start.51) | collective-permute-done | bytes 393248 | tf_op jit(solution)/shard_map/ppermute | solution.py:575
  366.4 2.1 collective-permute-done.54
  369.4 1.4 collective-permute-start.55
  370.8 2.8 collective-permute-start.56
  374.8 1.5 pad_maximum_fusion.1
  376.3 1.3 copy.57
  377.6 3.6 all-to-all-start.1
  381.2 4.0 collective-permute-done.56
  388.1 14.1 %all-to-all-done.1 = bf16[8,6,32,512]{3,2,1,0:T(8,128)(2,1)S(1)} async-done(((bf16[8,6,32,512]{3,2,1,0:T(8,128)(2,1)}), bf16[8,6,32,512]{3,2,1,0:T(8,128)(2,1)S(1)}, u32[]{:S(2)}, u32[]{:S(2)}) %all-to-all-start.1) | async-done | bytes 1572896 | tf_op jit(solution)/shard_map/all_to_all | solution.py:768
  (242 shorter events, 41.9 us)
Async XLA Ops:
  9.9 26.3 %all-to-all-start = ((bf16[8,2,3,32,512]{4,3,2,1,0:T(8,128)(2,1)}), bf16[8,2,3,32,512]{4,3,2,1,0:T(8,128)(2,1)S(1)}, u32[]{:S(2)}, u32[]{:S(2)}) async-start(bf16[8,2,3,32,512]{4,3,2,1,0:T(8,128)(2,1)} %pad_maximum_fusion), calls=%async_computation | async-start | bytes 3145728 | tf_op jit(solution)/shard_map/all_to_all | solution.py:665
  15.2 138.1 %all-gather.2.cloned.1.call-start = ((), (), s32[]{:S(2)}) async-start(), calls=%async_computation.4 | async-start | bytes 7864320 | tf_op jit(solution)/shard_map/all_gather | solution.py:670
  15.7 21.9 %collective-permute-start = (bf16[32,3200]{1,0:T(8,128)(2,1)S(1)}, bf16[32,3200]{1,0:T(8,128)(2,1)S(1)}, u32[]{:S(2)}, u32[]{:S(2)}) collective-permute-start(bf16[32,3200]{1,0:T(8,128)(2,1)S(1)} %concatenate.26), channel_id=1, source_target_pairs={{0,8},{1,9},{2,10},{3,11},{4,12},{5,13},{6,14},{7,15},{8,0},{9,1},... | collective-permute-start | bytes 614408 | tf_op jit(solution)/shard_map/ppermute | solution.py:575
  17.3 20.2 %collective-permute-start.1 = (bf16[32,3200]{1,0:T(8,128)(2,1)S(1)}, bf16[32,3200]{1,0:T(8,128)(2,1)S(1)}, u32[]{:S(2)}, u32[]{:S(2)}) collective-permute-start(bf16[32,3200]{1,0:T(8,128)(2,1)S(1)} %concatenate.26), channel_id=1, source_target_pairs={{0,16},{1,17},{2,18},{3,19},{4,20},{5,21},{6,22},{7,23},{8,24},{9,... | collective-permute-start | bytes 614408 | tf_op jit(solution)/shard_map/ppermute | solution.py:575
  19.9 17.7 %collective-permute-start.2 = (bf16[32,3200]{1,0:T(8,128)(2,1)S(1)}, bf16[32,3200]{1,0:T(8,128)(2,1)S(1)}, u32[]{:S(2)}, u32[]{:S(2)}) collective-permute-start(bf16[32,3200]{1,0:T(8,128)(2,1)S(1)} %concatenate.26), channel_id=1, source_target_pairs={{0,24},{1,25},{2,26},{3,27},{4,28},{5,29},{6,30},{7,31},{8,16},{9,... | collective-permute-start | bytes 614408 | tf_op jit(solution)/shard_map/ppermute | solution.py:575
  37.5 337.3 %reduce-scatter.3.cloned.1.call-start = ((), (), s32[]{:S(2)}) async-start(), calls=%async_computation.5 | async-start | bytes 2621440 | tf_op jit(solution)/shard_map/reduce_scatter | solution.py:715
  37.8 12.9 %collective-permute-start.7 = (bf16[4,32,1664]{2,1,0:T(8,128)(2,1)S(1)}, bf16[4,32,1664]{2,1,0:T(8,128)(2,1)S(1)}, u32[]{:S(2)}, u32[]{:S(2)}) collective-permute-start(bf16[4,32,1664]{2,1,0:T(8,128)(2,1)S(1)} %pad_maximum_fusion.5.refs_4_), channel_id=1, source_target_pairs={{0,4},{1,5},{2,6},{3,7},{4,0},{5,1},{6,2},{7,3},{8,12},{9,13},{10,... | collective-permute-start | bytes 1277960 | tf_op jit(solution)/shard_map/ppermute | solution.py:575
  38.5 12.1 %collective-permute-start.3 = (bf16[4,32,1536]{2,1,0:T(8,128)(2,1)S(1)}, bf16[4,32,1536]{2,1,0:T(8,128)(2,1)S(1)}, u32[]{:S(2)}, u32[]{:S(2)}) collective-permute-start(bf16[4,32,1536]{2,1,0:T(8,128)(2,1)S(1)} %pad_maximum_fusion.6.refs_0_), channel_id=1, source_target_pairs={{0,2},{1,3},{2,0},{3,1},{4,6},{5,7},{6,4},{7,5},{8,10},{9,11},{10,... | collective-permute-start | bytes 1179656 | tf_op jit(solution)/shard_map/ppermute | solution.py:575
  39.2 16.5 %collective-permute-start.4 = (bf16[4,32,1536]{2,1,0:T(8,128)(2,1)S(1)}, bf16[4,32,1536]{2,1,0:T(8,128)(2,1)S(1)}, u32[]{:S(2)}, u32[]{:S(2)}) collective-permute-start(bf16[4,32,1536]{2,1,0:T(8,128)(2,1)S(1)} %pad_maximum_fusion.6.refs_0_), channel_id=1, source_target_pairs={{0,4},{1,5},{2,6},{3,7},{4,0},{5,1},{6,2},{7,3},{8,12},{9,13},{10,... | collective-permute-start | bytes 1179656 | tf_op jit(solution)/shard_map/ppermute | solution.py:575
  40.6 16.1 %collective-permute-start.9 = (bf16[4,32,1536]{2,1,0:T(8,128)(2,1)S(1)}, bf16[4,32,1536]{2,1,0:T(8,128)(2,1)S(1)}, u32[]{:S(2)}, u32[]{:S(2)}) collective-permute-start(bf16[4,32,1536]{2,1,0:T(8,128)(2,1)S(1)} %pad_maximum_fusion.6.refs_0_), channel_id=1, source_target_pairs={{0,1},{1,0},{2,3},{3,2},{4,5},{5,4},{6,7},{7,6},{8,9},{9,8},{10,11... | collective-permute-start | bytes 1179656 | tf_op jit(solution)/shard_map/ppermute | solution.py:575
  40.6 19.2 %collective-permute-start.6 = (bf16[4,32,1664]{2,1,0:T(8,128)(2,1)S(1)}, bf16[4,32,1664]{2,1,0:T(8,128)(2,1)S(1)}, u32[]{:S(2)}, u32[]{:S(2)}) collective-permute-start(bf16[4,32,1664]{2,1,0:T(8,128)(2,1)S(1)} %pad_maximum_fusion.5.refs_4_), channel_id=1, source_target_pairs={{0,2},{1,3},{2,0},{3,1},{4,6},{5,7},{6,4},{7,5},{8,10},{9,11},{10,... | collective-permute-start | bytes 1277960 | tf_op jit(solution)/shard_map/ppermute | solution.py:575
  50.7 15.6 %collective-permute-start.8 = (bf16[4,32,1664]{2,1,0:T(8,128)(2,1)S(1)}, bf16[4,32,1664]{2,1,0:T(8,128)(2,1)S(1)}, u32[]{:S(2)}, u32[]{:S(2)}) collective-permute-start(bf16[4,32,1664]{2,1,0:T(8,128)(2,1)S(1)} %collective-permute-done.7.refs_6_), channel_id=1, source_target_pairs={{0,2},{1,3},{2,0},{3,1},{4,6},{5,7},{6,4},{7,5},{8,10},{9,11},{10,... | collective-permute-start | bytes 1277960 | tf_op jit(solution)/shard_map/ppermute | solution.py:575
  55.7 10.5 %collective-permute-start.5 = (bf16[4,32,1536]{2,1,0:T(8,128)(2,1)S(1)}, bf16[4,32,1536]{2,1,0:T(8,128)(2,1)S(1)}, u32[]{:S(2)}, u32[]{:S(2)}) collective-permute-start(bf16[4,32,1536]{2,1,0:T(8,128)(2,1)S(1)} %collective-permute-done.3.refs_1_), channel_id=1, source_target_pairs={{0,4},{1,5},{2,6},{3,7},{4,0},{5,1},{6,2},{7,3},{8,12},{9,13},{10,... | collective-permute-start | bytes 1179656 | tf_op jit(solution)/shard_map/ppermute | solution.py:575
  69.2 26.0 %collective-permute-start.17 = (bf16[512,1024]{1,0:T(8,128)(2,1)S(1)}, bf16[512,1024]{1,0:T(8,128)(2,1)S(1)}, u32[]{:S(2)}, u32[]{:S(2)}) collective-permute-start(bf16[512,1024]{1,0:T(8,128)(2,1)S(1)} %copy-done.4), channel_id=1, source_target_pairs={{0,2},{1,3},{2,0},{3,1},{4,6},{5,7},{6,4},{7,5},{8,10},{9,11},{10,... | collective-permute-start | bytes 3145736 | tf_op jit(solution)/shard_map/ppermute | solution.py:575
  71.3 24.9 %collective-permute-start.18 = (bf16[512,1024]{1,0:T(8,128)(2,1)S(1)}, bf16[512,1024]{1,0:T(8,128)(2,1)S(1)}, u32[]{:S(2)}, u32[]{:S(2)}) collective-permute-start(bf16[512,1024]{1,0:T(8,128)(2,1)S(1)} %copy-done.4), channel_id=1, source_target_pairs={{0,4},{1,5},{2,6},{3,7},{4,0},{5,1},{6,2},{7,3},{8,12},{9,13},{10,... | collective-permute-start | bytes 3145736 | tf_op jit(solution)/shard_map/ppermute | solution.py:575
  96.2 25.1 %collective-permute-start.19 = (bf16[528,1024]{1,0:T(8,128)(2,1)}, bf16[528,1024]{1,0:T(8,128)(2,1)S(1)}, u32[]{:S(2)}, u32[]{:S(2)}) collective-permute-start(bf16[528,1024]{1,0:T(8,128)(2,1)} %get-tuple-element.174.refs_8_.refs_6_), channel_id=1, source_target_pairs={{0,2},{1,3},{2,0},{3,1},{4,6},{5,7},{6,4},{7,5},{8,10},{9,11},{10,... | collective-permute-start | bytes 3244040 | tf_op jit(solution)/shard_map/ppermute | solution.py:575
  96.6 25.1 %collective-permute-start.20 = (bf16[528,1024]{1,0:T(8,128)(2,1)}, bf16[528,1024]{1,0:T(8,128)(2,1)S(1)}, u32[]{:S(2)}, u32[]{:S(2)}) collective-permute-start(bf16[528,1024]{1,0:T(8,128)(2,1)} %get-tuple-element.174.refs_8_.refs_6_), channel_id=1, source_target_pairs={{0,4},{1,5},{2,6},{3,7},{4,0},{5,1},{6,2},{7,3},{8,12},{9,13},{10,... | collective-permute-start | bytes 3244040 | tf_op jit(solution)/shard_map/ppermute | solution.py:575
  97.9 23.8 %collective-permute-start.21 = (bf16[528,1024]{1,0:T(8,128)(2,1)}, bf16[528,1024]{1,0:T(8,128)(2,1)}, u32[]{:S(2)}, u32[]{:S(2)}) collective-permute-start(bf16[528,1024]{1,0:T(8,128)(2,1)} %get-tuple-element.174.refs_8_.refs_6_), channel_id=1, source_target_pairs={{0,1},{1,0},{2,3},{3,2},{4,5},{5,4},{6,7},{7,6},{8,9},{9,8},{10,11... | collective-permute-start | bytes 3244040 | tf_op jit(solution)/shard_map/ppermute | solution.py:575
  121.9 23.4 %collective-permute-start.23 = (bf16[512,1024]{1,0:T(8,128)(2,1)S(1)}, bf16[512,1024]{1,0:T(8,128)(2,1)S(1)}, u32[]{:S(2)}, u32[]{:S(2)}) collective-permute-start(bf16[512,1024]{1,0:T(8,128)(2,1)S(1)} %pad_maximum_fusion.3), channel_id=1, source_target_pairs={{0,2},{1,3},{2,0},{3,1},{4,6},{5,7},{6,4},{7,5},{8,10},{9,11},{10,... | collective-permute-start | bytes 3145736 | tf_op jit(solution)/shard_map/ppermute | solution.py:575
  123.5 24.5 %collective-permute-start.24 = (bf16[528,1024]{1,0:T(8,128)(2,1)S(1)}, bf16[528,1024]{1,0:T(8,128)(2,1)S(1)}, u32[]{:S(2)}, u32[]{:S(2)}) collective-permute-start(bf16[528,1024]{1,0:T(8,128)(2,1)S(1)} %pad_maximum_fusion.2), channel_id=1, source_target_pairs={{0,4},{1,5},{2,6},{3,7},{4,0},{5,1},{6,2},{7,3},{8,12},{9,13},{10,... | collective-permute-start | bytes 3244040 | tf_op jit(solution)/shard_map/ppermute | solution.py:575
  124.8 23.1 %collective-permute-start.25 = (bf16[528,1024]{1,0:T(8,128)(2,1)S(1)}, bf16[528,1024]{1,0:T(8,128)(2,1)S(1)}, u32[]{:S(2)}, u32[]{:S(2)}) collective-permute-start(bf16[528,1024]{1,0:T(8,128)(2,1)S(1)} %collective-permute-done.19.refs_4_), channel_id=1, source_target_pairs={{0,1},{1,0},{2,3},{3,2},{4,5},{5,4},{6,7},{7,6},{8,9},{9,8},{10,11... | collective-permute-start | bytes 3244040 | tf_op jit(solution)/shard_map/ppermute | solution.py:575
  124.9 23.1 %collective-permute-start.27 = (bf16[528,1024]{1,0:T(8,128)(2,1)S(1)}, bf16[528,1024]{1,0:T(8,128)(2,1)S(1)}, u32[]{:S(2)}, u32[]{:S(2)}) collective-permute-start(bf16[528,1024]{1,0:T(8,128)(2,1)S(1)} %collective-permute-done.20.refs_10_), channel_id=1, source_target_pairs={{0,1},{1,0},{2,3},{3,2},{4,5},{5,4},{6,7},{7,6},{8,9},{9,8},{10,11... | collective-permute-start | bytes 3244040 | tf_op jit(solution)/shard_map/ppermute | solution.py:575
  125.4 20.0 %collective-permute-start.26 = (bf16[512,1024]{1,0:T(8,128)(2,1)S(1)}, bf16[512,1024]{1,0:T(8,128)(2,1)S(1)}, u32[]{:S(2)}, u32[]{:S(2)}) collective-permute-start(bf16[512,1024]{1,0:T(8,128)(2,1)S(1)} %collective-permute-done.17.refs_6_), channel_id=1, source_target_pairs={{0,1},{1,0},{2,3},{3,2},{4,5},{5,4},{6,7},{7,6},{8,9},{9,8},{10,11... | collective-permute-start | bytes 3145736 | tf_op jit(solution)/shard_map/ppermute | solution.py:575
  226.4 19.1 %collective-permute-start.36 = (bf16[512,1024]{1,0:T(8,128)(2,1)}, bf16[512,1024]{1,0:T(8,128)(2,1)}, u32[]{:S(2)}, u32[]{:S(2)}) collective-permute-start(bf16[512,1024]{1,0:T(8,128)(2,1)} %get-tuple-element.217), channel_id=1, source_target_pairs={{0,1},{1,0},{2,3},{3,2},{4,5},{5,4},{6,7},{7,6},{8,9},{9,8},{10,11... | collective-permute-start | bytes 3145736 | tf_op jit(solution)/shard_map/ppermute | solution.py:575
  226.6 19.0 %collective-permute-start.37 = (bf16[512,1024]{1,0:T(8,128)(2,1)}, bf16[512,1024]{1,0:T(8,128)(2,1)}, u32[]{:S(2)}, u32[]{:S(2)}) collective-permute-start(bf16[512,1024]{1,0:T(8,128)(2,1)} %get-tuple-element.218), channel_id=1, source_target_pairs={{0,1},{1,0},{2,3},{3,2},{4,5},{5,4},{6,7},{7,6},{8,9},{9,8},{10,11... | collective-permute-start | bytes 3145736 | tf_op jit(solution)/shard_map/ppermute | solution.py:575
  226.9 18.6 %collective-permute-start.38 = (bf16[512,1024]{1,0:T(8,128)(2,1)}, bf16[512,1024]{1,0:T(8,128)(2,1)}, u32[]{:S(2)}, u32[]{:S(2)}) collective-permute-start(bf16[512,1024]{1,0:T(8,128)(2,1)} %get-tuple-element.219), channel_id=1, source_target_pairs={{0,1},{1,0},{2,3},{3,2},{4,5},{5,4},{6,7},{7,6},{8,9},{9,8},{10,11... | collective-permute-start | bytes 3145736 | tf_op jit(solution)/shard_map/ppermute | solution.py:575
  227.1 18.4 %collective-permute-start.35 = (bf16[272,1024]{1,0:T(8,128)(2,1)S(1)}, bf16[272,1024]{1,0:T(8,128)(2,1)}, u32[]{:S(2)}, u32[]{:S(2)}) collective-permute-start(bf16[272,1024]{1,0:T(8,128)(2,1)S(1)} %add_convert_fusion.6), channel_id=1, source_target_pairs={{0,4},{1,5},{2,6},{3,7},{4,0},{5,1},{6,2},{7,3},{8,12},{9,13},{10,... | collective-permute-start | bytes 1671176 | tf_op jit(solution)/shard_map/ppermute | solution.py:575
  228.4 17.1 %collective-permute-start.34 = (bf16[256,1024]{1,0:T(8,128)(2,1)}, bf16[256,1024]{1,0:T(8,128)(2,1)}, u32[]{:S(2)}, u32[]{:S(2)}) collective-permute-start(bf16[256,1024]{1,0:T(8,128)(2,1)} %add_convert_fusion.8), channel_id=1, source_target_pairs={{0,2},{1,3},{2,0},{3,1},{4,6},{5,7},{6,4},{7,5},{8,10},{9,11},{10,... | collective-permute-start | bytes 1572872 | tf_op jit(solution)/shard_map/ppermute | solution.py:575
  245.6 129.2 %reduce-scatter.5.cloned.1.call-start = ((), (), s32[]{:S(2)}) async-start(), calls=%async_computation.6 | async-start | bytes 5242880 | tf_op jit(solution)/shard_map/reduce_scatter | solution.py:715
  250.6 30.4 %collective-permute-start.39 = (bf16[528,1024]{1,0:T(8,128)(2,1)}, bf16[528,1024]{1,0:T(8,128)(2,1)S(1)}, u32[]{:S(2)}, u32[]{:S(2)}) collective-permute-start(bf16[528,1024]{1,0:T(8,128)(2,1)} %add_convert_fusion.1), channel_id=1, source_target_pairs={{0,2},{1,3},{2,0},{3,1},{4,6},{5,7},{6,4},{7,5},{8,10},{9,11},{10,... | collective-permute-start | bytes 3244040 | tf_op jit(solution)/shard_map/ppermute | solution.py:575
  251.6 29.5 %collective-permute-start.40 = (bf16[528,1024]{1,0:T(8,128)(2,1)}, bf16[528,1024]{1,0:T(8,128)(2,1)}, u32[]{:S(2)}, u32[]{:S(2)}) collective-permute-start(bf16[528,1024]{1,0:T(8,128)(2,1)} %add_convert_fusion), channel_id=1, source_target_pairs={{0,4},{1,5},{2,6},{3,7},{4,0},{5,1},{6,2},{7,3},{8,12},{9,13},{10,... | collective-permute-start | bytes 3244040 | tf_op jit(solution)/shard_map/ppermute | solution.py:575
  252.3 28.7 %collective-permute-start.41 = (bf16[528,1024]{1,0:T(8,128)(2,1)}, bf16[528,1024]{1,0:T(8,128)(2,1)}, u32[]{:S(2)}, u32[]{:S(2)}) collective-permute-start(bf16[528,1024]{1,0:T(8,128)(2,1)} %get-tuple-element.266), channel_id=1, source_target_pairs={{0,1},{1,0},{2,3},{3,2},{4,5},{5,4},{6,7},{7,6},{8,9},{9,8},{10,11... | collective-permute-start | bytes 3244040 | tf_op jit(solution)/shard_map/ppermute | solution.py:575
  252.3 28.7 %collective-permute-start.42 = (bf16[512,1024]{1,0:T(8,128)(2,1)S(1)}, bf16[512,1024]{1,0:T(8,128)(2,1)}, u32[]{:S(2)}, u32[]{:S(2)}) collective-permute-start(bf16[512,1024]{1,0:T(8,128)(2,1)S(1)} %get-tuple-element.267), channel_id=1, source_target_pairs={{0,1},{1,0},{2,3},{3,2},{4,5},{5,4},{6,7},{7,6},{8,9},{9,8},{10,11... | collective-permute-start | bytes 3145736 | tf_op jit(solution)/shard_map/ppermute | solution.py:575
  283.5 37.4 %collective-permute-start.43 = (bf16[512,1024]{1,0:T(8,128)(2,1)}, bf16[512,1024]{1,0:T(8,128)(2,1)}, u32[]{:S(2)}, u32[]{:S(2)}) collective-permute-start(bf16[512,1024]{1,0:T(8,128)(2,1)} %get-tuple-element.299), channel_id=1, source_target_pairs={{0,2},{1,3},{2,0},{3,1},{4,6},{5,7},{6,4},{7,5},{8,10},{9,11},{10,... | collective-permute-start | bytes 3145736 | tf_op jit(solution)/shard_map/ppermute | solution.py:575
  284.5 36.4 %collective-permute-start.44 = (bf16[512,1024]{1,0:T(8,128)(2,1)}, bf16[512,1024]{1,0:T(8,128)(2,1)}, u32[]{:S(2)}, u32[]{:S(2)}) collective-permute-start(bf16[512,1024]{1,0:T(8,128)(2,1)} %get-tuple-element.300), channel_id=1, source_target_pairs={{0,4},{1,5},{2,6},{3,7},{4,0},{5,1},{6,2},{7,3},{8,12},{9,13},{10,... | collective-permute-start | bytes 3145736 | tf_op jit(solution)/shard_map/ppermute | solution.py:575
  285.9 35.0 %collective-permute-start.45 = (bf16[256,1024]{1,0:T(8,128)(2,1)}, bf16[256,1024]{1,0:T(8,128)(2,1)}, u32[]{:S(2)}, u32[]{:S(2)}) collective-permute-start(bf16[256,1024]{1,0:T(8,128)(2,1)} %get-tuple-element.301), channel_id=1, source_target_pairs={{0,6},{1,7},{2,4},{3,5},{4,2},{5,3},{6,0},{7,1},{8,14},{9,15},{10,... | collective-permute-start | bytes 1572872 | tf_op jit(solution)/shard_map/ppermute | solution.py:575
  320.9 13.9 %collective-permute-start.46 = (bf16[256,1024]{1,0:T(8,128)(2,1)S(1)}, bf16[256,1024]{1,0:T(8,128)(2,1)S(1)}, u32[]{:S(2)}, u32[]{:S(2)}) collective-permute-start(bf16[256,1024]{1,0:T(8,128)(2,1)S(1)} %get-tuple-element.306), channel_id=1, source_target_pairs={{0,6},{1,7},{2,4},{3,5},{4,2},{5,3},{6,0},{7,1},{8,14},{9,15},{10,... | collective-permute-start | bytes 1572872 | tf_op jit(solution)/shard_map/ppermute | solution.py:575
  322.6 13.6 %collective-permute-start.48 = (bf16[8,32,1536]{2,1,0:T(8,128)(2,1)}, bf16[8,32,1536]{2,1,0:T(8,128)(2,1)S(1)}, u32[]{:S(2)}, u32[]{:S(2)}) collective-permute-start(bf16[8,32,1536]{2,1,0:T(8,128)(2,1)} %get-tuple-element.311), channel_id=1, source_target_pairs={{0,1},{1,0},{2,3},{3,2},{4,5},{5,4},{6,7},{7,6},{8,9},{9,8},{10,11... | collective-permute-start | bytes 2359304 | tf_op jit(solution)/shard_map/ppermute | solution.py:575
  322.6 16.0 %collective-permute-start.47 = (bf16[8,32,1536]{2,1,0:T(8,128)(2,1)}, bf16[8,32,1536]{2,1,0:T(8,128)(2,1)S(1)}, u32[]{:S(2)}, u32[]{:S(2)}) collective-permute-start(bf16[8,32,1536]{2,1,0:T(8,128)(2,1)} %get-tuple-element.309), channel_id=1, source_target_pairs={{0,1},{1,0},{2,3},{3,2},{4,5},{5,4},{6,7},{7,6},{8,9},{9,8},{10,11... | collective-permute-start | bytes 2359304 | tf_op jit(solution)/shard_map/ppermute | solution.py:575
  323.1 13.3 %collective-permute-start.49 = (bf16[8,32,1664]{2,1,0:T(8,128)(2,1)}, bf16[8,32,1664]{2,1,0:T(8,128)(2,1)S(1)}, u32[]{:S(2)}, u32[]{:S(2)}) collective-permute-start(bf16[8,32,1664]{2,1,0:T(8,128)(2,1)} %get-tuple-element.313), channel_id=1, source_target_pairs={{0,1},{1,0},{2,3},{3,2},{4,5},{5,4},{6,7},{7,6},{8,9},{9,8},{10,11... | collective-permute-start | bytes 2555912 | tf_op jit(solution)/shard_map/ppermute | solution.py:575
  323.1 16.6 %collective-permute-start.52 = (bf16[8,32,1664]{2,1,0:T(8,128)(2,1)}, bf16[8,32,1664]{2,1,0:T(8,128)(2,1)S(1)}, u32[]{:S(2)}, u32[]{:S(2)}) collective-permute-start(bf16[8,32,1664]{2,1,0:T(8,128)(2,1)} %get-tuple-element.316), channel_id=1, source_target_pairs={{0,1},{1,0},{2,3},{3,2},{4,5},{5,4},{6,7},{7,6},{8,9},{9,8},{10,11... | collective-permute-start | bytes 2555912 | tf_op jit(solution)/shard_map/ppermute | solution.py:575
  337.5 17.7 %collective-permute-start.50 = (bf16[8,32,1536]{2,1,0:T(8,128)(2,1)S(1)}, bf16[8,32,1536]{2,1,0:T(8,128)(2,1)S(1)}, u32[]{:S(2)}, u32[]{:S(2)}) collective-permute-start(bf16[8,32,1536]{2,1,0:T(8,128)(2,1)S(1)} %add_convert_fusion.4), channel_id=1, source_target_pairs={{0,2},{1,3},{2,0},{3,1},{4,6},{5,7},{6,4},{7,5},{8,10},{9,11},{10,... | collective-permute-start | bytes 2359304 | tf_op jit(solution)/shard_map/ppermute | solution.py:575
  338.9 21.3 %collective-permute-start.53 = (bf16[8,32,1664]{2,1,0:T(8,128)(2,1)S(1)}, bf16[8,32,1664]{2,1,0:T(8,128)(2,1)S(1)}, u32[]{:S(2)}, u32[]{:S(2)}) collective-permute-start(bf16[8,32,1664]{2,1,0:T(8,128)(2,1)S(1)} %add_convert_fusion.3), channel_id=1, source_target_pairs={{0,4},{1,5},{2,6},{3,7},{4,0},{5,1},{6,2},{7,3},{8,12},{9,13},{10,... | collective-permute-start | bytes 2555912 | tf_op jit(solution)/shard_map/ppermute | solution.py:575
  355.4 10.9 %collective-permute-start.51 = (bf16[4,32,1536]{2,1,0:T(8,128)(2,1)S(1)}, bf16[4,32,1536]{2,1,0:T(8,128)(2,1)S(1)}, u32[]{:S(2)}, u32[]{:S(2)}) collective-permute-start(bf16[4,32,1536]{2,1,0:T(8,128)(2,1)S(1)} %add_convert_fusion.13), channel_id=1, source_target_pairs={{0,4},{1,5},{2,6},{3,7},{4,0},{5,1},{6,2},{7,3},{8,12},{9,13},{10,... | collective-permute-start | bytes 1179656 | tf_op jit(solution)/shard_map/ppermute | solution.py:575
  369.4 11.9 %collective-permute-start.55 = (bf16[32,3200]{1,0:T(8,128)(2,1)}, bf16[32,3200]{1,0:T(8,128)(2,1)S(1)}, u32[]{:S(2)}, u32[]{:S(2)}) collective-permute-start(bf16[32,3200]{1,0:T(8,128)(2,1)} %get-tuple-element.365), channel_id=1, source_target_pairs={{0,8},{1,9},{2,10},{3,11},{4,12},{5,13},{6,14},{7,15},{8,0},{9,1},... | collective-permute-start | bytes 614408 | tf_op jit(solution)/shard_map/ppermute | solution.py:575
  370.8 14.4 %collective-permute-start.56 = (bf16[32,3200]{1,0:T(8,128)(2,1)S(1)}, bf16[32,3200]{1,0:T(8,128)(2,1)S(1)}, u32[]{:S(2)}, u32[]{:S(2)}) collective-permute-start(bf16[32,3200]{1,0:T(8,128)(2,1)S(1)} %get-tuple-element.367), channel_id=1, source_target_pairs={{0,16},{1,17},{2,18},{3,19},{4,20},{5,21},{6,22},{7,23},{8,24},{9,... | collective-permute-start | bytes 614408 | tf_op jit(solution)/shard_map/ppermute | solution.py:575
  373.6 11.6 %collective-permute-start.57 = (bf16[32,3200]{1,0:T(8,128)(2,1)S(1)}, bf16[32,3200]{1,0:T(8,128)(2,1)S(1)}, u32[]{:S(2)}, u32[]{:S(2)}) collective-permute-start(bf16[32,3200]{1,0:T(8,128)(2,1)S(1)} %get-tuple-element.366), channel_id=1, source_target_pairs={{0,24},{1,25},{2,26},{3,27},{4,28},{5,29},{6,30},{7,31},{8,16},{9,... | collective-permute-start | bytes 614408 | tf_op jit(solution)/shard_map/ppermute | solution.py:575
  377.6 24.5 %all-to-all-start.1 = ((bf16[8,6,32,512]{3,2,1,0:T(8,128)(2,1)}), bf16[8,6,32,512]{3,2,1,0:T(8,128)(2,1)S(1)}, u32[]{:S(2)}, u32[]{:S(2)}) async-start(bf16[8,6,32,512]{3,2,1,0:T(8,128)(2,1)} %bitcast.56), calls=%async_computation.3 | async-start | bytes 3145728 | tf_op jit(solution)/shard_map/all_to_all | solution.py:768
  (65 other events, 590.7 us)
Sparse Core Ops, SparseCore 0:
  37.6 114.7 all-gather.1
  245.7 43.8 reduce-scatter.2
  292.0 76.0 reduce-scatter.4
where the time goes:
time: 417 us; the launch traced here: 413 us
  Pallas kernels  165 us (40%)
  waiting for transfers between devices  146 us (35%)
  starting transfers between devices  49.5 us (12%)
  other arithmetic  24.7 us (6%)
  between operations  15.1 us (4%)
  local copies, waits for them, and re-layouts  12.2 us (3%)
    ppermute x58, waiting for transfers between devices, swap(): return lax.ppermute(array, 'dp', [(i, i ^ offset) for i in range(n)])  118 us
    pallas_call x1, Pallas kernels, expert_call(): pl.pallas_call(functools.partial(expert_kernel, plan, len(arrays)), grid=...  66.9 us
    pallas_call x2, Pallas kernels, weight_grads(): pl.pallas_call(functools.partial(weight_grad_kernel, count, len(pairs), s...  44.2 us
    ppermute x58, starting transfers between devices, swap(): return lax.ppermute(array, 'dp', [(i, i ^ offset) for i in range(n)])  40.5 us
    pallas_call x1, Pallas kernels, backward_call(): pl.pallas_call(functools.partial(backward_kernel, spots), in_specs=[pl.Bl...  32.6 us
    pallas_call x1, Pallas kernels, forward_call(): pl.pallas_call(functools.partial(forward_kernel, spots), in_specs=[pl.Blo...  21.5 us
    all_to_all x1, waiting for transfers between devices, local(): lax.all_to_all(owned, 'dp', split_axis=0, concat_axis=0, axis_index_group...  14.1 us
    all_to_all x1, waiting for transfers between devices, local(): lax.all_to_all(expert_part, 'dp', split_axis=0, concat_axis=0, axis_index...  13.8 us
  transfers between devices with their start and end apart: 63, of which 25 were waited for; matrix products, arithmetic and copies ran while one was open for 6% of the time, Pallas kernels for 24%

commit v1 on v0

--- a/solution.py
+++ b/solution.py
@@ -602,7 +602,7 @@
 
     def dense_sum(pieces, earlier):
         if not pieced:
-            return up(lax.psum_scatter(pieces[0], "dp", scatter_dimension=0, tiled=True))
+            return lax.psum_scatter(up(pieces[0]), "dp", scatter_dimension=0, tiled=True)
 
         def add(a, b):
             return (up(a) + up(b)).astype(BF)
@@ -712,6 +712,8 @@
         second_plan = [pieces_of(8 + i, 12 + i) for i in range(4)]
 
         def outer_sum(grads):
+            if not pieced:
+                grads = up(grads)
             return lax.psum_scatter(grads, "dp", scatter_dimension=1, tiled=True, axis_index_groups=outer_groups)
 
         def with_core(block, other):

time: 417 us -> 417 us (level)
  no operation moved by 1% of the time
where the time goes in v1:
time: 417 us; the launch traced here: 413 us
  Pallas kernels  165 us (40%)
  waiting for transfers between devices  146 us (35%)
  starting transfers between devices  49.5 us (12%)
  other arithmetic  24.7 us (6%)
  between operations  15.1 us (4%)
  local copies, waits for them, and re-layouts  12.2 us (3%)
    ppermute x58, waiting for transfers between devices, swap(): return lax.ppermute(array, 'dp', [(i, i ^ offset) for i in range(n)])  118 us
    pallas_call x1, Pallas kernels, expert_call(): pl.pallas_call(functools.partial(expert_kernel, plan, len(arrays)), grid=...  66.9 us
    pallas_call x2, Pallas kernels, weight_grads(): pl.pallas_call(functools.partial(weight_grad_kernel, count, len(pairs), s...  44.2 us
    ppermute x58, starting transfers between devices, swap(): return lax.ppermute(array, 'dp', [(i, i ^ offset) for i in range(n)])  40.5 us
    pallas_call x1, Pallas kernels, backward_call(): pl.pallas_call(functools.partial(backward_kernel, spots), in_specs=[pl.Bl...  32.6 us
    pallas_call x1, Pallas kernels, forward_call(): pl.pallas_call(functools.partial(forward_kernel, spots), in_specs=[pl.Blo...  21.5 us
    all_to_all x1, waiting for transfers between devices, local(): lax.all_to_all(owned, 'dp', split_axis=0, concat_axis=0, axis_index_group...  14.1 us
    all_to_all x1, waiting for transfers between devices, local(): lax.all_to_all(expert_part, 'dp', split_axis=0, concat_axis=0, axis_index...  13.8 us
  transfers between devices with their start and end apart: 63, of which 25 were waited for; matrix products, arithmetic and copies ran while one was open for 6% of the time, Pallas kernels for 24%

profile of v1, /device:TPU:0, one launch (start us, length us, event | category | flops | bytes accessed | tf_op | source)
XLA Modules:
  0.0 412.7 jit_solution(9508597312555912811)
XLA Ops:
  7.2 2.7 pad_maximum_fusion
  9.9 5.3 %all-to-all-start = ((bf16[8,2,3,32,512]{4,3,2,1,0:T(8,128)(2,1)}), bf16[8,2,3,32,512]{4,3,2,1,0:T(8,128)(2,1)S(1)}, u32[]{:S(2)}, u32[]{:S(2)}) async-start(bf16[8,2,3,32,512]{4,3,2,1,0:T(8,128)(2,1)} %pad_maximum_fusion), calls=%async_computation | async-start | bytes 3145728 | tf_op jit(solution)/shard_map/all_to_all | solution.py:665
  15.7 1.6 collective-permute-start
  17.3 2.6 collective-permute-start.1
  22.4 13.8 %all-to-all-done = bf16[8,2,3,32,512]{4,3,2,1,0:T(8,128)(2,1)S(1)} async-done(((bf16[8,2,3,32,512]{4,3,2,1,0:T(8,128)(2,1)}), bf16[8,2,3,32,512]{4,3,2,1,0:T(8,128)(2,1)S(1)}, u32[]{:S(2)}, u32[]{:S(2)}) %all-to-all-start) | async-done | bytes 1572896 | tf_op jit(solution)/shard_map/all_to_all | solution.py:665
  39.2 1.4 collective-permute-start.4
  40.6 1.5 collective-permute-start.6
  42.1 8.6 %collective-permute-done.3.refs_1_ = bf16[4,32,1536]{2,1,0:T(8,128)(2,1)S(1)} collective-permute-done((bf16[4,32,1536]{2,1,0:T(8,128)(2,1)S(1)}, bf16[4,32,1536]{2,1,0:T(8,128)(2,1)S(1)}, u32[]{:S(2)}, u32[]{:S(2)}) %collective-permute-start.3) | collective-permute-done | bytes 393248 | tf_op jit(solution)/shard_map/ppermute | solution.py:575
  51.3 4.4 %collective-permute-done.4.refs_2_ = bf16[4,32,1536]{2,1,0:T(8,128)(2,1)S(1)} collective-permute-done((bf16[4,32,1536]{2,1,0:T(8,128)(2,1)S(1)}, bf16[4,32,1536]{2,1,0:T(8,128)(2,1)S(1)}, u32[]{:S(2)}, u32[]{:S(2)}) %collective-permute-start.4) | collective-permute-done | bytes 393248 | tf_op jit(solution)/shard_map/ppermute | solution.py:575
  57.5 2.3 collective-permute-done.6.refs_5_
  60.3 5.9 %collective-permute-done.8.refs_7_ = bf16[4,32,1664]{2,1,0:T(8,128)(2,1)S(1)} collective-permute-done((bf16[4,32,1664]{2,1,0:T(8,128)(2,1)S(1)}, bf16[4,32,1664]{2,1,0:T(8,128)(2,1)S(1)}, u32[]{:S(2)}, u32[]{:S(2)}) %collective-permute-start.8) | collective-permute-done | bytes 426016 | tf_op jit(solution)/shard_map/ppermute | solution.py:575
  66.8 1.7 collective-permute-done.11.refs_10_
  69.2 2.2 collective-permute-start.17
  71.3 1.3 collective-permute-start.18
  73.6 21.5 %shard_map.229 = (f32[4,4,512]{2,1,0:T(4,128)}, bf16[528,1024]{1,0:T(8,128)(2,1)}, bf16[1024,3200]{1,0:T(8,128)(2,1)}, bf16[512,1024]{1,0:T(8,128)(2,1)}, bf16[5...) custom-call(s32[1]{0:T(128)} %bitcast.me_ref, ...), custom_call_target="tpu_custom_call" | custom-call | flops 1 | bytes 1 | tf_op jit(solution)/shard_map/pallas_call | solution.py:179
  96.6 1.3 collective-permute-start.20
  98.4 3.7 collective-permute-done.22.refs_13_
  102.1 19.2 %collective-permute-done.19.refs_4_ = bf16[528,1024]{1,0:T(8,128)(2,1)S(1)} collective-permute-done((bf16[528,1024]{1,0:T(8,128)(2,1)}, bf16[528,1024]{1,0:T(8,128)(2,1)S(1)}, u32[]{:S(2)}, u32[]{:S(2)}) %collective-permute-start.19) | collective-permute-done | bytes 1081376 | tf_op jit(solution)/shard_map/ppermute | solution.py:575
  121.9 1.4 collective-permute-start.23
  123.5 1.4 collective-permute-start.24
  125.4 19.9 %collective-permute-done.23.refs_0_ = bf16[512,1024]{1,0:T(8,128)(2,1)S(1)} collective-permute-done((bf16[512,1024]{1,0:T(8,128)(2,1)S(1)}, bf16[512,1024]{1,0:T(8,128)(2,1)S(1)}, u32[]{:S(2)}, u32[]{:S(2)}) %collective-permute-start.23) | collective-permute-done | bytes 1048608 | tf_op jit(solution)/shard_map/ppermute | solution.py:575
  145.3 2.6 collective-permute-done.28.refs_15_
  148.6 3.7 collective-permute-done.29.refs_1_
  153.3 66.9 %shard_map.230 = (bf16[4096,512]{1,0:T(8,128)(2,1)}, bf16[4096,512]{1,0:T(8,128)(2,1)}, bf16[4096,512]{1,0:T(8,128)(2,1)}, bf16[4096,512]{1,0:T(8,128)(2,1)}, bf...) custom-call(s32[1]{0:T(128)S(6)} %rem.18.place_ref, ...), custom_call_target="tpu_custom_call" | custom-call | flops 1 | bytes 1 | tf_op jit(solution)/shard_map/pallas_call | solution.py:473
  220.9 2.3 collective-permute-done.31
  223.2 2.0 add_convert_fusion.8
  227.1 1.3 collective-permute-start.35
  229.4 16.1 %shard_map.231 = (bf16[2,1024,512]{2,1,0:T(8,128)(2,1)}, bf16[528,1024]{1,0:T(8,128)(2,1)}, bf16[528,1024]{1,0:T(8,128)(2,1)}) custom-call(bf16[4096,1024]{1,0:T(8,128)(2,1)} %get-tuple-element.205.left_ref, bf16[4096,512]{1,0:T(8,128)(2,1)} %get-tuple-element.206.refs_0_, bf16[4096,512]{1,0:T(8,128)(2,1)} %get-tuple-element.207.refs_1_, ...), custom_call_target="tpu_custom_call" | custom-call | flops 1 | bytes 1 | tf_op jit(solution)/shard_map/pallas_call | solution.py:540
  245.6 2.7 add_convert_fusion
  248.3 2.3 add_convert_fusion.1
  252.8 28.2 %shard_map.232 = (bf16[4,1024,512]{2,1,0:T(8,128)(2,1)}, bf16[512,1024]{1,0:T(8,128)(2,1)}, bf16[512,1024]{1,0:T(8,128)(2,1)}, bf16[512,1024]{1,0:T(8,128)(2,1)}) custom-call(bf16[4096,1024]{1,0:T(8,128)(2,1)} %get-tuple-element.252.left_ref, bf16[4096,512]{1,0:T(8,128)(2,1)} %get-tuple-element.253.refs_0_, bf16[4096,512]{1,0:T(8,128)(2,1)} %get-tuple-element.254.refs_1_, ...), custom_call_target="tpu_custom_call" | custom-call | flops 1 | bytes 1 | tf_op jit(solution)/shard_map/pallas_call | solution.py:540
  284.5 1.3 collective-permute-start.44
  287.0 32.6 %shard_map.233 = (f32[512,1024]{1,0:T(8,128)}, bf16[8,32,1536]{2,1,0:T(8,128)(2,1)}, bf16[8,32,1536]{2,1,0:T(8,128)(2,1)}, bf16[8,32,1664]{2,1,0:T(8,128)(2,1)},...) custom-call(s32[1]{0:T(128)} %bitcast.me_ref, ...), custom_call_target="tpu_custom_call" | custom-call | flops 1 | bytes 1 | tf_op jit(solution)/shard_map/pallas_call | solution.py:342
  320.9 1.7 collective-permute-start.46
  323.6 2.8 convert_add_fusion
  326.5 8.3 %collective-permute-done.46 = bf16[256,1024]{1,0:T(8,128)(2,1)S(1)} collective-permute-done((bf16[256,1024]{1,0:T(8,128)(2,1)S(1)}, bf16[256,1024]{1,0:T(8,128)(2,1)S(1)}, u32[]{:S(2)}, u32[]{:S(2)}) %collective-permute-start.46) | collective-permute-done | bytes 524320 | tf_op jit(solution)/shard_map/ppermute | solution.py:575
  334.8 1.4 fusion
  339.9 15.3 %collective-permute-done.50 = bf16[8,32,1536]{2,1,0:T(8,128)(2,1)S(1)} collective-permute-done((bf16[8,32,1536]{2,1,0:T(8,128)(2,1)S(1)}, bf16[8,32,1536]{2,1,0:T(8,128)(2,1)S(1)}, u32[]{:S(2)}, u32[]{:S(2)}) %collective-permute-start.50) | collective-permute-done | bytes 786464 | tf_op jit(solution)/shard_map/ppermute | solution.py:575
  355.8 4.3 %collective-permute-done.53 = bf16[8,32,1664]{2,1,0:T(8,128)(2,1)S(1)} collective-permute-done((bf16[8,32,1664]{2,1,0:T(8,128)(2,1)S(1)}, bf16[8,32,1664]{2,1,0:T(8,128)(2,1)S(1)}, u32[]{:S(2)}, u32[]{:S(2)}) %collective-permute-start.53) | collective-permute-done | bytes 852000 | tf_op jit(solution)/shard_map/ppermute | solution.py:575
  360.8 5.5 %collective-permute-done.51 = bf16[4,32,1536]{2,1,0:T(8,128)(2,1)S(1)} collective-permute-done((bf16[4,32,1536]{2,1,0:T(8,128)(2,1)S(1)}, bf16[4,32,1536]{2,1,0:T(8,128)(2,1)S(1)}, u32[]{:S(2)}, u32[]{:S(2)}) %collective-permute-start.51) | collective-permute-done | bytes 393248 | tf_op jit(solution)/shard_map/ppermute | solution.py:575
  366.4 2.1 collective-permute-done.54
  369.4 1.4 collective-permute-start.55
  370.8 2.8 collective-permute-start.56
  374.8 1.5 pad_maximum_fusion.1
  376.3 1.3 copy.57
  377.6 3.6 all-to-all-start.1
  381.2 4.0 collective-permute-done.56
  388.1 14.1 %all-to-all-done.1 = bf16[8,6,32,512]{3,2,1,0:T(8,128)(2,1)S(1)} async-done(((bf16[8,6,32,512]{3,2,1,0:T(8,128)(2,1)}), bf16[8,6,32,512]{3,2,1,0:T(8,128)(2,1)S(1)}, u32[]{:S(2)}, u32[]{:S(2)}) %all-to-all-start.1) | async-done | bytes 1572896 | tf_op jit(solution)/shard_map/all_to_all | solution.py:770
  (242 shorter events, 41.9 us)
Async XLA Ops:
  9.9 26.3 %all-to-all-start = ((bf16[8,2,3,32,512]{4,3,2,1,0:T(8,128)(2,1)}), bf16[8,2,3,32,512]{4,3,2,1,0:T(8,128)(2,1)S(1)}, u32[]{:S(2)}, u32[]{:S(2)}) async-start(bf16[8,2,3,32,512]{4,3,2,1,0:T(8,128)(2,1)} %pad_maximum_fusion), calls=%async_computation | async-start | bytes 3145728 | tf_op jit(solution)/shard_map/all_to_all | solution.py:665
  15.2 138.1 %all-gather.2.cloned.1.call-start = ((), (), s32[]{:S(2)}) async-start(), calls=%async_computation.4 | async-start | bytes 7864320 | tf_op jit(solution)/shard_map/all_gather | solution.py:670
  15.7 21.9 %collective-permute-start = (bf16[32,3200]{1,0:T(8,128)(2,1)S(1)}, bf16[32,3200]{1,0:T(8,128)(2,1)S(1)}, u32[]{:S(2)}, u32[]{:S(2)}) collective-permute-start(bf16[32,3200]{1,0:T(8,128)(2,1)S(1)} %concatenate.26), channel_id=1, source_target_pairs={{0,8},{1,9},{2,10},{3,11},{4,12},{5,13},{6,14},{7,15},{8,0},{9,1},... | collective-permute-start | bytes 614408 | tf_op jit(solution)/shard_map/ppermute | solution.py:575
  17.3 20.2 %collective-permute-start.1 = (bf16[32,3200]{1,0:T(8,128)(2,1)S(1)}, bf16[32,3200]{1,0:T(8,128)(2,1)S(1)}, u32[]{:S(2)}, u32[]{:S(2)}) collective-permute-start(bf16[32,3200]{1,0:T(8,128)(2,1)S(1)} %concatenate.26), channel_id=1, source_target_pairs={{0,16},{1,17},{2,18},{3,19},{4,20},{5,21},{6,22},{7,23},{8,24},{9,... | collective-permute-start | bytes 614408 | tf_op jit(solution)/shard_map/ppermute | solution.py:575
  19.9 17.7 %collective-permute-start.2 = (bf16[32,3200]{1,0:T(8,128)(2,1)S(1)}, bf16[32,3200]{1,0:T(8,128)(2,1)S(1)}, u32[]{:S(2)}, u32[]{:S(2)}) collective-permute-start(bf16[32,3200]{1,0:T(8,128)(2,1)S(1)} %concatenate.26), channel_id=1, source_target_pairs={{0,24},{1,25},{2,26},{3,27},{4,28},{5,29},{6,30},{7,31},{8,16},{9,... | collective-permute-start | bytes 614408 | tf_op jit(solution)/shard_map/ppermute | solution.py:575
  37.5 337.3 %reduce-scatter.3.cloned.1.call-start = ((), (), s32[]{:S(2)}) async-start(), calls=%async_computation.5 | async-start | bytes 2621440 | tf_op jit(solution)/shard_map/reduce_scatter | solution.py:717
  37.8 12.9 %collective-permute-start.7 = (bf16[4,32,1664]{2,1,0:T(8,128)(2,1)S(1)}, bf16[4,32,1664]{2,1,0:T(8,128)(2,1)S(1)}, u32[]{:S(2)}, u32[]{:S(2)}) collective-permute-start(bf16[4,32,1664]{2,1,0:T(8,128)(2,1)S(1)} %pad_maximum_fusion.5.refs_4_), channel_id=1, source_target_pairs={{0,4},{1,5},{2,6},{3,7},{4,0},{5,1},{6,2},{7,3},{8,12},{9,13},{10,... | collective-permute-start | bytes 1277960 | tf_op jit(solution)/shard_map/ppermute | solution.py:575
  38.5 12.1 %collective-permute-start.3 = (bf16[4,32,1536]{2,1,0:T(8,128)(2,1)S(1)}, bf16[4,32,1536]{2,1,0:T(8,128)(2,1)S(1)}, u32[]{:S(2)}, u32[]{:S(2)}) collective-permute-start(bf16[4,32,1536]{2,1,0:T(8,128)(2,1)S(1)} %pad_maximum_fusion.6.refs_0_), channel_id=1, source_target_pairs={{0,2},{1,3},{2,0},{3,1},{4,6},{5,7},{6,4},{7,5},{8,10},{9,11},{10,... | collective-permute-start | bytes 1179656 | tf_op jit(solution)/shard_map/ppermute | solution.py:575
  39.2 16.5 %collective-permute-start.4 = (bf16[4,32,1536]{2,1,0:T(8,128)(2,1)S(1)}, bf16[4,32,1536]{2,1,0:T(8,128)(2,1)S(1)}, u32[]{:S(2)}, u32[]{:S(2)}) collective-permute-start(bf16[4,32,1536]{2,1,0:T(8,128)(2,1)S(1)} %pad_maximum_fusion.6.refs_0_), channel_id=1, source_target_pairs={{0,4},{1,5},{2,6},{3,7},{4,0},{5,1},{6,2},{7,3},{8,12},{9,13},{10,... | collective-permute-start | bytes 1179656 | tf_op jit(solution)/shard_map/ppermute | solution.py:575
  40.6 16.1 %collective-permute-start.9 = (bf16[4,32,1536]{2,1,0:T(8,128)(2,1)S(1)}, bf16[4,32,1536]{2,1,0:T(8,128)(2,1)S(1)}, u32[]{:S(2)}, u32[]{:S(2)}) collective-permute-start(bf16[4,32,1536]{2,1,0:T(8,128)(2,1)S(1)} %pad_maximum_fusion.6.refs_0_), channel_id=1, source_target_pairs={{0,1},{1,0},{2,3},{3,2},{4,5},{5,4},{6,7},{7,6},{8,9},{9,8},{10,11... | collective-permute-start | bytes 1179656 | tf_op jit(solution)/shard_map/ppermute | solution.py:575
  40.6 19.2 %collective-permute-start.6 = (bf16[4,32,1664]{2,1,0:T(8,128)(2,1)S(1)}, bf16[4,32,1664]{2,1,0:T(8,128)(2,1)S(1)}, u32[]{:S(2)}, u32[]{:S(2)}) collective-permute-start(bf16[4,32,1664]{2,1,0:T(8,128)(2,1)S(1)} %pad_maximum_fusion.5.refs_4_), channel_id=1, source_target_pairs={{0,2},{1,3},{2,0},{3,1},{4,6},{5,7},{6,4},{7,5},{8,10},{9,11},{10,... | collective-permute-start | bytes 1277960 | tf_op jit(solution)/shard_map/ppermute | solution.py:575
  50.7 15.6 %collective-permute-start.8 = (bf16[4,32,1664]{2,1,0:T(8,128)(2,1)S(1)}, bf16[4,32,1664]{2,1,0:T(8,128)(2,1)S(1)}, u32[]{:S(2)}, u32[]{:S(2)}) collective-permute-start(bf16[4,32,1664]{2,1,0:T(8,128)(2,1)S(1)} %collective-permute-done.7.refs_6_), channel_id=1, source_target_pairs={{0,2},{1,3},{2,0},{3,1},{4,6},{5,7},{6,4},{7,5},{8,10},{9,11},{10,... | collective-permute-start | bytes 1277960 | tf_op jit(solution)/shard_map/ppermute | solution.py:575
  55.7 10.5 %collective-permute-start.5 = (bf16[4,32,1536]{2,1,0:T(8,128)(2,1)S(1)}, bf16[4,32,1536]{2,1,0:T(8,128)(2,1)S(1)}, u32[]{:S(2)}, u32[]{:S(2)}) collective-permute-start(bf16[4,32,1536]{2,1,0:T(8,128)(2,1)S(1)} %collective-permute-done.3.refs_1_), channel_id=1, source_target_pairs={{0,4},{1,5},{2,6},{3,7},{4,0},{5,1},{6,2},{7,3},{8,12},{9,13},{10,... | collective-permute-start | bytes 1179656 | tf_op jit(solution)/shard_map/ppermute | solution.py:575
  69.2 26.0 %collective-permute-start.17 = (bf16[512,1024]{1,0:T(8,128)(2,1)S(1)}, bf16[512,1024]{1,0:T(8,128)(2,1)S(1)}, u32[]{:S(2)}, u32[]{:S(2)}) collective-permute-start(bf16[512,1024]{1,0:T(8,128)(2,1)S(1)} %copy-done.4), channel_id=1, source_target_pairs={{0,2},{1,3},{2,0},{3,1},{4,6},{5,7},{6,4},{7,5},{8,10},{9,11},{10,... | collective-permute-start | bytes 3145736 | tf_op jit(solution)/shard_map/ppermute | solution.py:575
  71.3 24.9 %collective-permute-start.18 = (bf16[512,1024]{1,0:T(8,128)(2,1)S(1)}, bf16[512,1024]{1,0:T(8,128)(2,1)S(1)}, u32[]{:S(2)}, u32[]{:S(2)}) collective-permute-start(bf16[512,1024]{1,0:T(8,128)(2,1)S(1)} %copy-done.4), channel_id=1, source_target_pairs={{0,4},{1,5},{2,6},{3,7},{4,0},{5,1},{6,2},{7,3},{8,12},{9,13},{10,... | collective-permute-start | bytes 3145736 | tf_op jit(solution)/shard_map/ppermute | solution.py:575
  96.2 25.1 %collective-permute-start.19 = (bf16[528,1024]{1,0:T(8,128)(2,1)}, bf16[528,1024]{1,0:T(8,128)(2,1)S(1)}, u32[]{:S(2)}, u32[]{:S(2)}) collective-permute-start(bf16[528,1024]{1,0:T(8,128)(2,1)} %get-tuple-element.174.refs_8_.refs_6_), channel_id=1, source_target_pairs={{0,2},{1,3},{2,0},{3,1},{4,6},{5,7},{6,4},{7,5},{8,10},{9,11},{10,... | collective-permute-start | bytes 3244040 | tf_op jit(solution)/shard_map/ppermute | solution.py:575
  96.6 25.1 %collective-permute-start.20 = (bf16[528,1024]{1,0:T(8,128)(2,1)}, bf16[528,1024]{1,0:T(8,128)(2,1)S(1)}, u32[]{:S(2)}, u32[]{:S(2)}) collective-permute-start(bf16[528,1024]{1,0:T(8,128)(2,1)} %get-tuple-element.174.refs_8_.refs_6_), channel_id=1, source_target_pairs={{0,4},{1,5},{2,6},{3,7},{4,0},{5,1},{6,2},{7,3},{8,12},{9,13},{10,... | collective-permute-start | bytes 3244040 | tf_op jit(solution)/shard_map/ppermute | solution.py:575
  97.9 23.8 %collective-permute-start.21 = (bf16[528,1024]{1,0:T(8,128)(2,1)}, bf16[528,1024]{1,0:T(8,128)(2,1)}, u32[]{:S(2)}, u32[]{:S(2)}) collective-permute-start(bf16[528,1024]{1,0:T(8,128)(2,1)} %get-tuple-element.174.refs_8_.refs_6_), channel_id=1, source_target_pairs={{0,1},{1,0},{2,3},{3,2},{4,5},{5,4},{6,7},{7,6},{8,9},{9,8},{10,11... | collective-permute-start | bytes 3244040 | tf_op jit(solution)/shard_map/ppermute | solution.py:575
  121.9 23.4 %collective-permute-start.23 = (bf16[512,1024]{1,0:T(8,128)(2,1)S(1)}, bf16[512,1024]{1,0:T(8,128)(2,1)S(1)}, u32[]{:S(2)}, u32[]{:S(2)}) collective-permute-start(bf16[512,1024]{1,0:T(8,128)(2,1)S(1)} %pad_maximum_fusion.3), channel_id=1, source_target_pairs={{0,2},{1,3},{2,0},{3,1},{4,6},{5,7},{6,4},{7,5},{8,10},{9,11},{10,... | collective-permute-start | bytes 3145736 | tf_op jit(solution)/shard_map/ppermute | solution.py:575
  123.5 24.5 %collective-permute-start.24 = (bf16[528,1024]{1,0:T(8,128)(2,1)S(1)}, bf16[528,1024]{1,0:T(8,128)(2,1)S(1)}, u32[]{:S(2)}, u32[]{:S(2)}) collective-permute-start(bf16[528,1024]{1,0:T(8,128)(2,1)S(1)} %pad_maximum_fusion.2), channel_id=1, source_target_pairs={{0,4},{1,5},{2,6},{3,7},{4,0},{5,1},{6,2},{7,3},{8,12},{9,13},{10,... | collective-permute-start | bytes 3244040 | tf_op jit(solution)/shard_map/ppermute | solution.py:575
  124.8 23.1 %collective-permute-start.25 = (bf16[528,1024]{1,0:T(8,128)(2,1)S(1)}, bf16[528,1024]{1,0:T(8,128)(2,1)S(1)}, u32[]{:S(2)}, u32[]{:S(2)}) collective-permute-start(bf16[528,1024]{1,0:T(8,128)(2,1)S(1)} %collective-permute-done.19.refs_4_), channel_id=1, source_target_pairs={{0,1},{1,0},{2,3},{3,2},{4,5},{5,4},{6,7},{7,6},{8,9},{9,8},{10,11... | collective-permute-start | bytes 3244040 | tf_op jit(solution)/shard_map/ppermute | solution.py:575
  124.9 23.1 %collective-permute-start.27 = (bf16[528,1024]{1,0:T(8,128)(2,1)S(1)}, bf16[528,1024]{1,0:T(8,128)(2,1)S(1)}, u32[]{:S(2)}, u32[]{:S(2)}) collective-permute-start(bf16[528,1024]{1,0:T(8,128)(2,1)S(1)} %collective-permute-done.20.refs_10_), channel_id=1, source_target_pairs={{0,1},{1,0},{2,3},{3,2},{4,5},{5,4},{6,7},{7,6},{8,9},{9,8},{10,11... | collective-permute-start | bytes 3244040 | tf_op jit(solution)/shard_map/ppermute | solution.py:575
  125.4 20.0 %collective-permute-start.26 = (bf16[512,1024]{1,0:T(8,128)(2,1)S(1)}, bf16[512,1024]{1,0:T(8,128)(2,1)S(1)}, u32[]{:S(2)}, u32[]{:S(2)}) collective-permute-start(bf16[512,1024]{1,0:T(8,128)(2,1)S(1)} %collective-permute-done.17.refs_6_), channel_id=1, source_target_pairs={{0,1},{1,0},{2,3},{3,2},{4,5},{5,4},{6,7},{7,6},{8,9},{9,8},{10,11... | collective-permute-start | bytes 3145736 | tf_op jit(solution)/shard_map/ppermute | solution.py:575
  226.4 19.1 %collective-permute-start.36 = (bf16[512,1024]{1,0:T(8,128)(2,1)}, bf16[512,1024]{1,0:T(8,128)(2,1)}, u32[]{:S(2)}, u32[]{:S(2)}) collective-permute-start(bf16[512,1024]{1,0:T(8,128)(2,1)} %get-tuple-element.217), channel_id=1, source_target_pairs={{0,1},{1,0},{2,3},{3,2},{4,5},{5,4},{6,7},{7,6},{8,9},{9,8},{10,11... | collective-permute-start | bytes 3145736 | tf_op jit(solution)/shard_map/ppermute | solution.py:575
  226.6 19.0 %collective-permute-start.37 = (bf16[512,1024]{1,0:T(8,128)(2,1)}, bf16[512,1024]{1,0:T(8,128)(2,1)}, u32[]{:S(2)}, u32[]{:S(2)}) collective-permute-start(bf16[512,1024]{1,0:T(8,128)(2,1)} %get-tuple-element.218), channel_id=1, source_target_pairs={{0,1},{1,0},{2,3},{3,2},{4,5},{5,4},{6,7},{7,6},{8,9},{9,8},{10,11... | collective-permute-start | bytes 3145736 | tf_op jit(solution)/shard_map/ppermute | solution.py:575
  226.9 18.6 %collective-permute-start.38 = (bf16[512,1024]{1,0:T(8,128)(2,1)}, bf16[512,1024]{1,0:T(8,128)(2,1)}, u32[]{:S(2)}, u32[]{:S(2)}) collective-permute-start(bf16[512,1024]{1,0:T(8,128)(2,1)} %get-tuple-element.219), channel_id=1, source_target_pairs={{0,1},{1,0},{2,3},{3,2},{4,5},{5,4},{6,7},{7,6},{8,9},{9,8},{10,11... | collective-permute-start | bytes 3145736 | tf_op jit(solution)/shard_map/ppermute | solution.py:575
  227.1 18.4 %collective-permute-start.35 = (bf16[272,1024]{1,0:T(8,128)(2,1)S(1)}, bf16[272,1024]{1,0:T(8,128)(2,1)}, u32[]{:S(2)}, u32[]{:S(2)}) collective-permute-start(bf16[272,1024]{1,0:T(8,128)(2,1)S(1)} %add_convert_fusion.6), channel_id=1, source_target_pairs={{0,4},{1,5},{2,6},{3,7},{4,0},{5,1},{6,2},{7,3},{8,12},{9,13},{10,... | collective-permute-start | bytes 1671176 | tf_op jit(solution)/shard_map/ppermute | solution.py:575
  228.4 17.1 %collective-permute-start.34 = (bf16[256,1024]{1,0:T(8,128)(2,1)}, bf16[256,1024]{1,0:T(8,128)(2,1)}, u32[]{:S(2)}, u32[]{:S(2)}) collective-permute-start(bf16[256,1024]{1,0:T(8,128)(2,1)} %add_convert_fusion.8), channel_id=1, source_target_pairs={{0,2},{1,3},{2,0},{3,1},{4,6},{5,7},{6,4},{7,5},{8,10},{9,11},{10,... | collective-permute-start | bytes 1572872 | tf_op jit(solution)/shard_map/ppermute | solution.py:575
  245.6 129.2 %reduce-scatter.5.cloned.1.call-start = ((), (), s32[]{:S(2)}) async-start(), calls=%async_computation.6 | async-start | bytes 5242880 | tf_op jit(solution)/shard_map/reduce_scatter | solution.py:717
  250.6 30.4 %collective-permute-start.39 = (bf16[528,1024]{1,0:T(8,128)(2,1)}, bf16[528,1024]{1,0:T(8,128)(2,1)S(1)}, u32[]{:S(2)}, u32[]{:S(2)}) collective-permute-start(bf16[528,1024]{1,0:T(8,128)(2,1)} %add_convert_fusion.1), channel_id=1, source_target_pairs={{0,2},{1,3},{2,0},{3,1},{4,6},{5,7},{6,4},{7,5},{8,10},{9,11},{10,... | collective-permute-start | bytes 3244040 | tf_op jit(solution)/shard_map/ppermute | solution.py:575
  251.6 29.5 %collective-permute-start.40 = (bf16[528,1024]{1,0:T(8,128)(2,1)}, bf16[528,1024]{1,0:T(8,128)(2,1)}, u32[]{:S(2)}, u32[]{:S(2)}) collective-permute-start(bf16[528,1024]{1,0:T(8,128)(2,1)} %add_convert_fusion), channel_id=1, source_target_pairs={{0,4},{1,5},{2,6},{3,7},{4,0},{5,1},{6,2},{7,3},{8,12},{9,13},{10,... | collective-permute-start | bytes 3244040 | tf_op jit(solution)/shard_map/ppermute | solution.py:575
  252.3 28.7 %collective-permute-start.41 = (bf16[528,1024]{1,0:T(8,128)(2,1)}, bf16[528,1024]{1,0:T(8,128)(2,1)}, u32[]{:S(2)}, u32[]{:S(2)}) collective-permute-start(bf16[528,1024]{1,0:T(8,128)(2,1)} %get-tuple-element.266), channel_id=1, source_target_pairs={{0,1},{1,0},{2,3},{3,2},{4,5},{5,4},{6,7},{7,6},{8,9},{9,8},{10,11... | collective-permute-start | bytes 3244040 | tf_op jit(solution)/shard_map/ppermute | solution.py:575
  252.3 28.7 %collective-permute-start.42 = (bf16[512,1024]{1,0:T(8,128)(2,1)S(1)}, bf16[512,1024]{1,0:T(8,128)(2,1)}, u32[]{:S(2)}, u32[]{:S(2)}) collective-permute-start(bf16[512,1024]{1,0:T(8,128)(2,1)S(1)} %get-tuple-element.267), channel_id=1, source_target_pairs={{0,1},{1,0},{2,3},{3,2},{4,5},{5,4},{6,7},{7,6},{8,9},{9,8},{10,11... | collective-permute-start | bytes 3145736 | tf_op jit(solution)/shard_map/ppermute | solution.py:575
  283.5 37.4 %collective-permute-start.43 = (bf16[512,1024]{1,0:T(8,128)(2,1)}, bf16[512,1024]{1,0:T(8,128)(2,1)}, u32[]{:S(2)}, u32[]{:S(2)}) collective-permute-start(bf16[512,1024]{1,0:T(8,128)(2,1)} %get-tuple-element.299), channel_id=1, source_target_pairs={{0,2},{1,3},{2,0},{3,1},{4,6},{5,7},{6,4},{7,5},{8,10},{9,11},{10,... | collective-permute-start | bytes 3145736 | tf_op jit(solution)/shard_map/ppermute | solution.py:575
  284.5 36.4 %collective-permute-start.44 = (bf16[512,1024]{1,0:T(8,128)(2,1)}, bf16[512,1024]{1,0:T(8,128)(2,1)}, u32[]{:S(2)}, u32[]{:S(2)}) collective-permute-start(bf16[512,1024]{1,0:T(8,128)(2,1)} %get-tuple-element.300), channel_id=1, source_target_pairs={{0,4},{1,5},{2,6},{3,7},{4,0},{5,1},{6,2},{7,3},{8,12},{9,13},{10,... | collective-permute-start | bytes 3145736 | tf_op jit(solution)/shard_map/ppermute | solution.py:575
  285.9 35.0 %collective-permute-start.45 = (bf16[256,1024]{1,0:T(8,128)(2,1)}, bf16[256,1024]{1,0:T(8,128)(2,1)}, u32[]{:S(2)}, u32[]{:S(2)}) collective-permute-start(bf16[256,1024]{1,0:T(8,128)(2,1)} %get-tuple-element.301), channel_id=1, source_target_pairs={{0,6},{1,7},{2,4},{3,5},{4,2},{5,3},{6,0},{7,1},{8,14},{9,15},{10,... | collective-permute-start | bytes 1572872 | tf_op jit(solution)/shard_map/ppermute | solution.py:575
  320.9 13.9 %collective-permute-start.46 = (bf16[256,1024]{1,0:T(8,128)(2,1)S(1)}, bf16[256,1024]{1,0:T(8,128)(2,1)S(1)}, u32[]{:S(2)}, u32[]{:S(2)}) collective-permute-start(bf16[256,1024]{1,0:T(8,128)(2,1)S(1)} %get-tuple-element.306), channel_id=1, source_target_pairs={{0,6},{1,7},{2,4},{3,5},{4,2},{5,3},{6,0},{7,1},{8,14},{9,15},{10,... | collective-permute-start | bytes 1572872 | tf_op jit(solution)/shard_map/ppermute | solution.py:575
  322.6 13.6 %collective-permute-start.48 = (bf16[8,32,1536]{2,1,0:T(8,128)(2,1)}, bf16[8,32,1536]{2,1,0:T(8,128)(2,1)S(1)}, u32[]{:S(2)}, u32[]{:S(2)}) collective-permute-start(bf16[8,32,1536]{2,1,0:T(8,128)(2,1)} %get-tuple-element.311), channel_id=1, source_target_pairs={{0,1},{1,0},{2,3},{3,2},{4,5},{5,4},{6,7},{7,6},{8,9},{9,8},{10,11... | collective-permute-start | bytes 2359304 | tf_op jit(solution)/shard_map/ppermute | solution.py:575
  322.6 16.0 %collective-permute-start.47 = (bf16[8,32,1536]{2,1,0:T(8,128)(2,1)}, bf16[8,32,1536]{2,1,0:T(8,128)(2,1)S(1)}, u32[]{:S(2)}, u32[]{:S(2)}) collective-permute-start(bf16[8,32,1536]{2,1,0:T(8,128)(2,1)} %get-tuple-element.309), channel_id=1, source_target_pairs={{0,1},{1,0},{2,3},{3,2},{4,5},{5,4},{6,7},{7,6},{8,9},{9,8},{10,11... | collective-permute-start | bytes 2359304 | tf_op jit(solution)/shard_map/ppermute | solution.py:575
  323.1 13.3 %collective-permute-start.49 = (bf16[8,32,1664]{2,1,0:T(8,128)(2,1)}, bf16[8,32,1664]{2,1,0:T(8,128)(2,1)S(1)}, u32[]{:S(2)}, u32[]{:S(2)}) collective-permute-start(bf16[8,32,1664]{2,1,0:T(8,128)(2,1)} %get-tuple-element.313), channel_id=1, source_target_pairs={{0,1},{1,0},{2,3},{3,2},{4,5},{5,4},{6,7},{7,6},{8,9},{9,8},{10,11... | collective-permute-start | bytes 2555912 | tf_op jit(solution)/shard_map/ppermute | solution.py:575
  323.1 16.6 %collective-permute-start.52 = (bf16[8,32,1664]{2,1,0:T(8,128)(2,1)}, bf16[8,32,1664]{2,1,0:T(8,128)(2,1)S(1)}, u32[]{:S(2)}, u32[]{:S(2)}) collective-permute-start(bf16[8,32,1664]{2,1,0:T(8,128)(2,1)} %get-tuple-element.316), channel_id=1, source_target_pairs={{0,1},{1,0},{2,3},{3,2},{4,5},{5,4},{6,7},{7,6},{8,9},{9,8},{10,11... | collective-permute-start | bytes 2555912 | tf_op jit(solution)/shard_map/ppermute | solution.py:575
  337.5 17.7 %collective-permute-start.50 = (bf16[8,32,1536]{2,1,0:T(8,128)(2,1)S(1)}, bf16[8,32,1536]{2,1,0:T(8,128)(2,1)S(1)}, u32[]{:S(2)}, u32[]{:S(2)}) collective-permute-start(bf16[8,32,1536]{2,1,0:T(8,128)(2,1)S(1)} %add_convert_fusion.4), channel_id=1, source_target_pairs={{0,2},{1,3},{2,0},{3,1},{4,6},{5,7},{6,4},{7,5},{8,10},{9,11},{10,... | collective-permute-start | bytes 2359304 | tf_op jit(solution)/shard_map/ppermute | solution.py:575
  338.9 21.3 %collective-permute-start.53 = (bf16[8,32,1664]{2,1,0:T(8,128)(2,1)S(1)}, bf16[8,32,1664]{2,1,0:T(8,128)(2,1)S(1)}, u32[]{:S(2)}, u32[]{:S(2)}) collective-permute-start(bf16[8,32,1664]{2,1,0:T(8,128)(2,1)S(1)} %add_convert_fusion.3), channel_id=1, source_target_pairs={{0,4},{1,5},{2,6},{3,7},{4,0},{5,1},{6,2},{7,3},{8,12},{9,13},{10,... | collective-permute-start | bytes 2555912 | tf_op jit(solution)/shard_map/ppermute | solution.py:575
  355.4 10.9 %collective-permute-start.51 = (bf16[4,32,1536]{2,1,0:T(8,128)(2,1)S(1)}, bf16[4,32,1536]{2,1,0:T(8,128)(2,1)S(1)}, u32[]{:S(2)}, u32[]{:S(2)}) collective-permute-start(bf16[4,32,1536]{2,1,0:T(8,128)(2,1)S(1)} %add_convert_fusion.13), channel_id=1, source_target_pairs={{0,4},{1,5},{2,6},{3,7},{4,0},{5,1},{6,2},{7,3},{8,12},{9,13},{10,... | collective-permute-start | bytes 1179656 | tf_op jit(solution)/shard_map/ppermute | solution.py:575
  369.4 11.9 %collective-permute-start.55 = (bf16[32,3200]{1,0:T(8,128)(2,1)}, bf16[32,3200]{1,0:T(8,128)(2,1)S(1)}, u32[]{:S(2)}, u32[]{:S(2)}) collective-permute-start(bf16[32,3200]{1,0:T(8,128)(2,1)} %get-tuple-element.365), channel_id=1, source_target_pairs={{0,8},{1,9},{2,10},{3,11},{4,12},{5,13},{6,14},{7,15},{8,0},{9,1},... | collective-permute-start | bytes 614408 | tf_op jit(solution)/shard_map/ppermute | solution.py:575
  370.8 14.4 %collective-permute-start.56 = (bf16[32,3200]{1,0:T(8,128)(2,1)S(1)}, bf16[32,3200]{1,0:T(8,128)(2,1)S(1)}, u32[]{:S(2)}, u32[]{:S(2)}) collective-permute-start(bf16[32,3200]{1,0:T(8,128)(2,1)S(1)} %get-tuple-element.367), channel_id=1, source_target_pairs={{0,16},{1,17},{2,18},{3,19},{4,20},{5,21},{6,22},{7,23},{8,24},{9,... | collective-permute-start | bytes 614408 | tf_op jit(solution)/shard_map/ppermute | solution.py:575
  373.6 11.6 %collective-permute-start.57 = (bf16[32,3200]{1,0:T(8,128)(2,1)S(1)}, bf16[32,3200]{1,0:T(8,128)(2,1)S(1)}, u32[]{:S(2)}, u32[]{:S(2)}) collective-permute-start(bf16[32,3200]{1,0:T(8,128)(2,1)S(1)} %get-tuple-element.366), channel_id=1, source_target_pairs={{0,24},{1,25},{2,26},{3,27},{4,28},{5,29},{6,30},{7,31},{8,16},{9,... | collective-permute-start | bytes 614408 | tf_op jit(solution)/shard_map/ppermute | solution.py:575
  377.6 24.5 %all-to-all-start.1 = ((bf16[8,6,32,512]{3,2,1,0:T(8,128)(2,1)}), bf16[8,6,32,512]{3,2,1,0:T(8,128)(2,1)S(1)}, u32[]{:S(2)}, u32[]{:S(2)}) async-start(bf16[8,6,32,512]{3,2,1,0:T(8,128)(2,1)} %bitcast.56), calls=%async_computation.3 | async-start | bytes 3145728 | tf_op jit(solution)/shard_map/all_to_all | solution.py:770
  (65 other events, 590.7 us)
Sparse Core Ops, SparseCore 0:
  37.6 114.7 all-gather.1
  245.7 43.8 reduce-scatter.2
  292.0 76.0 reduce-scatter.4

commit v2 on v1

--- a/solution.py
+++ b/solution.py
@@ -600,9 +600,9 @@
                     spots.append(([core + far + d + k for d in (0, minor) for k in along_z], first))
         return shapes, spots
 
-    def dense_sum(pieces, earlier):
+    def dense_sum(pieces, earlier, packed):
         if not pieced:
-            return lax.psum_scatter(up(pieces[0]), "dp", scatter_dimension=0, tiled=True)
+            return lax.psum_scatter(up(pieces[0]), "dp", scatter_dimension=0, tiled=True), packed
 
         def add(a, b):
             return (up(a) + up(b)).astype(BF)
@@ -614,10 +614,11 @@
         left = add(add(near_l[:4], got_l[:4]), swap(sent_l, 4))
         right = add(add(near_r[:4], got_r[:4]), swap(sent_r, 2))
         both = jnp.concatenate([left, right], axis=2)
+        both, packed = lax.optimization_barrier((both, packed))
         total = up(both[0])
         for k in range(1, 4):
             total = total + up(swap(both[k], PLANE * k))
-        return total
+        return total, packed
 
     def both_cores(same_core):
         return [b for part in same_core for b in (part, swap(part, 1))]
@@ -764,8 +765,10 @@
         got_out_low = swap(out_xy[1], 6)
         output = r1 + up(out[4]) + up(out_core_own) + up(got_out[0]) + up(got_out[1])
         output_top, output_low = (output[top] + up(got_out[2])).astype(BF), output[low]
-        owned = jnp.concatenate([sums_d, sums_gu], axis=0).reshape(3 * MINE, PLANE, share, ff).transpose(1, 0, 2, 3)
-        dense_grads = dense_sum(grad_pieces, (got_out_low, output_top, output_low))
+        owned = jnp.concatenate(
+            [s.reshape(-1, PLANE, share, ff).transpose(1, 0, 2, 3) for s in (sums_d, sums_gu)], axis=1
+        )
+        dense_grads, owned = dense_sum(grad_pieces, (got_out_low, output_top, output_low), owned)
         output = jnp.concatenate([output_top, (output_low + up(got_out_low)).astype(BF)], axis=0)
         owned = lax.all_to_all(owned, "dp", split_axis=0, concat_axis=0, axis_index_groups=plane_groups)
 

time: 417 us -> 419 us (level)
    all_to_all x1, waiting for transfers between devices: 14.1 us -> 8.4 us  [local(): lax.all_to_all(owned, 'dp', split_axis=0, concat_axis=0, axis_index_group...]
  transfers between devices with their start and end apart: 63 -> 63, of which waited for: 25 -> 25; matrix products, arithmetic and copies ran while one was open for 6% -> 7% of each run, Pallas kernels for 24% -> 24%
where the time goes in v2:
time: 419 us; the launch traced here: 415 us
  Pallas kernels  165 us (39%)
  waiting for transfers between devices  143 us (34%)
  starting transfers between devices  49.4 us (12%)
  other arithmetic  27.5 us (7%)
  between operations  15.1 us (4%)
  local copies, waits for them, and re-layouts  14.1 us (3%)
    ppermute x58, waiting for transfers between devices, swap(): return lax.ppermute(array, 'dp', [(i, i ^ offset) for i in range(n)])  121 us
    pallas_call x1, Pallas kernels, expert_call(): pl.pallas_call(functools.partial(expert_kernel, plan, len(arrays)), grid=...  66.9 us
    pallas_call x2, Pallas kernels, weight_grads(): pl.pallas_call(functools.partial(weight_grad_kernel, count, len(pairs), s...  44.2 us
    ppermute x58, starting transfers between devices, swap(): return lax.ppermute(array, 'dp', [(i, i ^ offset) for i in range(n)])  40.3 us
    pallas_call x1, Pallas kernels, backward_call(): pl.pallas_call(functools.partial(backward_kernel, spots), in_specs=[pl.Bl...  32.6 us
    pallas_call x1, Pallas kernels, forward_call(): pl.pallas_call(functools.partial(forward_kernel, spots), in_specs=[pl.Blo...  21.5 us
    all_to_all x1, waiting for transfers between devices, local(): lax.all_to_all(expert_part, 'dp', split_axis=0, concat_axis=0, axis_index...  13.8 us
    all_to_all x1, waiting for transfers between devices, local(): lax.all_to_all(owned, 'dp', split_axis=0, concat_axis=0, axis_index_group...  8.4 us
  transfers between devices with their start and end apart: 63, of which 25 were waited for; matrix products, arithmetic and copies ran while one was open for 7% of the time, Pallas kernels for 24%

profile of v2, /device:TPU:0, one launch (start us, length us, event | category | flops | bytes accessed | tf_op | source)
XLA Modules:
  0.0 414.6 jit_solution(8096494126310653980)
XLA Ops:
  7.2 2.7 pad_maximum_fusion
  9.9 5.3 %all-to-all-start = ((bf16[8,2,3,32,512]{4,3,2,1,0:T(8,128)(2,1)}), bf16[8,2,3,32,512]{4,3,2,1,0:T(8,128)(2,1)S(1)}, u32[]{:S(2)}, u32[]{:S(2)}) async-start(bf16[8,2,3,32,512]{4,3,2,1,0:T(8,128)(2,1)} %pad_maximum_fusion), calls=%async_computation | async-start | bytes 3145728 | tf_op jit(solution)/shard_map/all_to_all | solution.py:666
  15.7 1.6 collective-permute-start
  17.3 2.6 collective-permute-start.1
  21.2 1.3 pad_maximum_fusion.8
  22.4 13.8 %all-to-all-done = bf16[8,2,3,32,512]{4,3,2,1,0:T(8,128)(2,1)S(1)} async-done(((bf16[8,2,3,32,512]{4,3,2,1,0:T(8,128)(2,1)}), bf16[8,2,3,32,512]{4,3,2,1,0:T(8,128)(2,1)S(1)}, u32[]{:S(2)}, u32[]{:S(2)}) %all-to-all-start) | async-done | bytes 1572896 | tf_op jit(solution)/shard_map/all_to_all | solution.py:666
  39.2 1.4 collective-permute-start.4
  40.6 1.5 collective-permute-start.6
  42.1 8.6 %collective-permute-done.3.refs_1_ = bf16[4,32,1536]{2,1,0:T(8,128)(2,1)S(1)} collective-permute-done((bf16[4,32,1536]{2,1,0:T(8,128)(2,1)S(1)}, bf16[4,32,1536]{2,1,0:T(8,128)(2,1)S(1)}, u32[]{:S(2)}, u32[]{:S(2)}) %collective-permute-start.3) | collective-permute-done | bytes 393248 | tf_op jit(solution)/shard_map/ppermute | solution.py:575
  51.3 4.4 %collective-permute-done.4.refs_2_ = bf16[4,32,1536]{2,1,0:T(8,128)(2,1)S(1)} collective-permute-done((bf16[4,32,1536]{2,1,0:T(8,128)(2,1)S(1)}, bf16[4,32,1536]{2,1,0:T(8,128)(2,1)S(1)}, u32[]{:S(2)}, u32[]{:S(2)}) %collective-permute-start.4) | collective-permute-done | bytes 393248 | tf_op jit(solution)/shard_map/ppermute | solution.py:575
  57.5 2.3 collective-permute-done.6.refs_5_
  60.3 5.9 %collective-permute-done.8.refs_7_ = bf16[4,32,1664]{2,1,0:T(8,128)(2,1)S(1)} collective-permute-done((bf16[4,32,1664]{2,1,0:T(8,128)(2,1)S(1)}, bf16[4,32,1664]{2,1,0:T(8,128)(2,1)S(1)}, u32[]{:S(2)}, u32[]{:S(2)}) %collective-permute-start.8) | collective-permute-done | bytes 426016 | tf_op jit(solution)/shard_map/ppermute | solution.py:575
  66.8 1.7 collective-permute-done.11.refs_10_
  69.2 2.2 collective-permute-start.17
  71.3 1.3 collective-permute-start.18
  73.6 21.5 %shard_map.229 = (f32[4,4,512]{2,1,0:T(4,128)}, bf16[528,1024]{1,0:T(8,128)(2,1)}, bf16[1024,3200]{1,0:T(8,128)(2,1)}, bf16[512,1024]{1,0:T(8,128)(2,1)}, bf16[5...) custom-call(s32[1]{0:T(128)} %bitcast.me_ref, ...), custom_call_target="tpu_custom_call" | custom-call | flops 1 | bytes 1 | tf_op jit(solution)/shard_map/pallas_call | solution.py:179
  96.6 1.3 collective-permute-start.20
  98.4 3.7 collective-permute-done.22.refs_13_
  102.1 19.2 %collective-permute-done.19.refs_4_ = bf16[528,1024]{1,0:T(8,128)(2,1)S(1)} collective-permute-done((bf16[528,1024]{1,0:T(8,128)(2,1)}, bf16[528,1024]{1,0:T(8,128)(2,1)S(1)}, u32[]{:S(2)}, u32[]{:S(2)}) %collective-permute-start.19) | collective-permute-done | bytes 1081376 | tf_op jit(solution)/shard_map/ppermute | solution.py:575
  121.9 1.4 collective-permute-start.23
  123.5 1.4 collective-permute-start.24
  125.4 19.9 %collective-permute-done.23.refs_0_ = bf16[512,1024]{1,0:T(8,128)(2,1)S(1)} collective-permute-done((bf16[512,1024]{1,0:T(8,128)(2,1)S(1)}, bf16[512,1024]{1,0:T(8,128)(2,1)S(1)}, u32[]{:S(2)}, u32[]{:S(2)}) %collective-permute-start.23) | collective-permute-done | bytes 1048608 | tf_op jit(solution)/shard_map/ppermute | solution.py:575
  145.3 2.6 collective-permute-done.28.refs_15_
  148.6 3.7 collective-permute-done.29.refs_1_
  153.3 66.9 %shard_map.230 = (bf16[4096,512]{1,0:T(8,128)(2,1)}, bf16[4096,512]{1,0:T(8,128)(2,1)}, bf16[4096,512]{1,0:T(8,128)(2,1)}, bf16[4096,512]{1,0:T(8,128)(2,1)}, bf...) custom-call(s32[1]{0:T(128)S(6)} %rem.18.place_ref, ...), custom_call_target="tpu_custom_call" | custom-call | flops 1 | bytes 1 | tf_op jit(solution)/shard_map/pallas_call | solution.py:473
  220.9 2.3 collective-permute-done.31
  223.2 2.0 add_convert_fusion.8
  227.1 1.3 collective-permute-start.35
  229.4 16.0 %shard_map.231 = (bf16[2,1024,512]{2,1,0:T(8,128)(2,1)}, bf16[528,1024]{1,0:T(8,128)(2,1)}, bf16[528,1024]{1,0:T(8,128)(2,1)}) custom-call(bf16[4096,1024]{1,0:T(8,128)(2,1)} %get-tuple-element.207.left_ref, bf16[4096,512]{1,0:T(8,128)(2,1)} %get-tuple-element.208.refs_0_, bf16[4096,512]{1,0:T(8,128)(2,1)} %get-tuple-element.209.refs_1_, ...), custom_call_target="tpu_custom_call" | custom-call | flops 1 | bytes 1 | tf_op jit(solution)/shard_map/pallas_call | solution.py:540
  245.6 2.7 add_convert_fusion
  248.3 2.3 add_convert_fusion.1
  252.8 28.1 %shard_map.232 = (bf16[4,1024,512]{2,1,0:T(8,128)(2,1)}, bf16[512,1024]{1,0:T(8,128)(2,1)}, bf16[512,1024]{1,0:T(8,128)(2,1)}, bf16[512,1024]{1,0:T(8,128)(2,1)}) custom-call(bf16[4096,1024]{1,0:T(8,128)(2,1)} %get-tuple-element.254.left_ref, bf16[4096,512]{1,0:T(8,128)(2,1)} %get-tuple-element.255.refs_0_, bf16[4096,512]{1,0:T(8,128)(2,1)} %get-tuple-element.256.refs_1_, ...), custom_call_target="tpu_custom_call" | custom-call | flops 1 | bytes 1 | tf_op jit(solution)/shard_map/pallas_call | solution.py:540
  284.5 1.3 collective-permute-start.44
  286.9 32.6 %shard_map.233 = (f32[512,1024]{1,0:T(8,128)}, bf16[8,32,1536]{2,1,0:T(8,128)(2,1)}, bf16[8,32,1536]{2,1,0:T(8,128)(2,1)}, bf16[8,32,1664]{2,1,0:T(8,128)(2,1)},...) custom-call(s32[1]{0:T(128)} %bitcast.me_ref, ...), custom_call_target="tpu_custom_call" | custom-call | flops 1 | bytes 1 | tf_op jit(solution)/shard_map/pallas_call | solution.py:342
  320.8 1.7 collective-permute-start.46
  323.6 2.8 convert_add_fusion
  326.4 8.3 %collective-permute-done.46 = bf16[256,1024]{1,0:T(8,128)(2,1)S(1)} collective-permute-done((bf16[256,1024]{1,0:T(8,128)(2,1)S(1)}, bf16[256,1024]{1,0:T(8,128)(2,1)S(1)}, u32[]{:S(2)}, u32[]{:S(2)}) %collective-permute-start.46) | collective-permute-done | bytes 524320 | tf_op jit(solution)/shard_map/ppermute | solution.py:575
  334.7 1.4 fusion
  339.8 15.3 %collective-permute-done.50 = bf16[8,32,1536]{2,1,0:T(8,128)(2,1)S(1)} collective-permute-done((bf16[8,32,1536]{2,1,0:T(8,128)(2,1)S(1)}, bf16[8,32,1536]{2,1,0:T(8,128)(2,1)S(1)}, u32[]{:S(2)}, u32[]{:S(2)}) %collective-permute-start.50) | collective-permute-done | bytes 786464 | tf_op jit(solution)/shard_map/ppermute | solution.py:575
  355.8 4.4 %collective-permute-done.53 = bf16[8,32,1664]{2,1,0:T(8,128)(2,1)S(1)} collective-permute-done((bf16[8,32,1664]{2,1,0:T(8,128)(2,1)S(1)}, bf16[8,32,1664]{2,1,0:T(8,128)(2,1)S(1)}, u32[]{:S(2)}, u32[]{:S(2)}) %collective-permute-start.53) | collective-permute-done | bytes 852000 | tf_op jit(solution)/shard_map/ppermute | solution.py:575
  361.4 4.9 %collective-permute-done.51 = bf16[4,32,1536]{2,1,0:T(8,128)(2,1)S(1)} collective-permute-done((bf16[4,32,1536]{2,1,0:T(8,128)(2,1)S(1)}, bf16[4,32,1536]{2,1,0:T(8,128)(2,1)S(1)}, u32[]{:S(2)}, u32[]{:S(2)}) %collective-permute-start.51) | collective-permute-done | bytes 393248 | tf_op jit(solution)/shard_map/ppermute | solution.py:575
  370.7 1.3 copy.59
  372.1 1.3 pad_maximum_fusion.1
  374.2 1.3 collective-permute-start.55
  375.5 2.9 collective-permute-start.56
  379.6 3.6 all-to-all-start.1
  383.2 8.6 %collective-permute-done.56 = bf16[32,3200]{1,0:T(8,128)(2,1)} collective-permute-done((bf16[32,3200]{1,0:T(8,128)(2,1)}, bf16[32,3200]{1,0:T(8,128)(2,1)}, u32[]{:S(2)}, u32[]{:S(2)}) %collective-permute-start.56) | collective-permute-done | bytes 204832 | tf_op jit(solution)/shard_map/ppermute | solution.py:575
  395.8 8.4 %all-to-all-done.1 = bf16[8,6,32,512]{3,2,1,0:T(8,128)(2,1)S(1)} async-done(((bf16[8,6,32,512]{3,2,1,0:T(8,128)(2,1)}), bf16[8,6,32,512]{3,2,1,0:T(8,128)(2,1)S(1)}, u32[]{:S(2)}, u32[]{:S(2)}) %all-to-all-start.1) | async-done | bytes 1572896 | tf_op jit(solution)/shard_map/all_to_all | solution.py:773
  (246 shorter events, 46.7 us)
Async XLA Ops:
  9.9 26.3 %all-to-all-start = ((bf16[8,2,3,32,512]{4,3,2,1,0:T(8,128)(2,1)}), bf16[8,2,3,32,512]{4,3,2,1,0:T(8,128)(2,1)S(1)}, u32[]{:S(2)}, u32[]{:S(2)}) async-start(bf16[8,2,3,32,512]{4,3,2,1,0:T(8,128)(2,1)} %pad_maximum_fusion), calls=%async_computation | async-start | bytes 3145728 | tf_op jit(solution)/shard_map/all_to_all | solution.py:666
  15.2 138.1 %all-gather.2.cloned.1.call-start = ((), (), s32[]{:S(2)}) async-start(), calls=%async_computation.4 | async-start | bytes 7864320 | tf_op jit(solution)/shard_map/all_gather | solution.py:671
  15.7 21.9 %collective-permute-start = (bf16[32,3200]{1,0:T(8,128)(2,1)S(1)}, bf16[32,3200]{1,0:T(8,128)(2,1)S(1)}, u32[]{:S(2)}, u32[]{:S(2)}) collective-permute-start(bf16[32,3200]{1,0:T(8,128)(2,1)S(1)} %concatenate.26), channel_id=1, source_target_pairs={{0,8},{1,9},{2,10},{3,11},{4,12},{5,13},{6,14},{7,15},{8,0},{9,1},... | collective-permute-start | bytes 614408 | tf_op jit(solution)/shard_map/ppermute | solution.py:575
  17.3 20.2 %collective-permute-start.1 = (bf16[32,3200]{1,0:T(8,128)(2,1)S(1)}, bf16[32,3200]{1,0:T(8,128)(2,1)S(1)}, u32[]{:S(2)}, u32[]{:S(2)}) collective-permute-start(bf16[32,3200]{1,0:T(8,128)(2,1)S(1)} %concatenate.26), channel_id=1, source_target_pairs={{0,16},{1,17},{2,18},{3,19},{4,20},{5,21},{6,22},{7,23},{8,24},{9,... | collective-permute-start | bytes 614408 | tf_op jit(solution)/shard_map/ppermute | solution.py:575
  19.9 17.7 %collective-permute-start.2 = (bf16[32,3200]{1,0:T(8,128)(2,1)S(1)}, bf16[32,3200]{1,0:T(8,128)(2,1)S(1)}, u32[]{:S(2)}, u32[]{:S(2)}) collective-permute-start(bf16[32,3200]{1,0:T(8,128)(2,1)S(1)} %concatenate.26), channel_id=1, source_target_pairs={{0,24},{1,25},{2,26},{3,27},{4,28},{5,29},{6,30},{7,31},{8,16},{9,... | collective-permute-start | bytes 614408 | tf_op jit(solution)/shard_map/ppermute | solution.py:575
  37.5 329.6 %reduce-scatter.3.cloned.1.call-start = ((), (), s32[]{:S(2)}) async-start(), calls=%async_computation.5 | async-start | bytes 2621440 | tf_op jit(solution)/shard_map/reduce_scatter | solution.py:718
  37.8 12.9 %collective-permute-start.7 = (bf16[4,32,1664]{2,1,0:T(8,128)(2,1)S(1)}, bf16[4,32,1664]{2,1,0:T(8,128)(2,1)S(1)}, u32[]{:S(2)}, u32[]{:S(2)}) collective-permute-start(bf16[4,32,1664]{2,1,0:T(8,128)(2,1)S(1)} %pad_maximum_fusion.6.refs_4_), channel_id=1, source_target_pairs={{0,4},{1,5},{2,6},{3,7},{4,0},{5,1},{6,2},{7,3},{8,12},{9,13},{10,... | collective-permute-start | bytes 1277960 | tf_op jit(solution)/shard_map/ppermute | solution.py:575
  38.5 12.1 %collective-permute-start.3 = (bf16[4,32,1536]{2,1,0:T(8,128)(2,1)S(1)}, bf16[4,32,1536]{2,1,0:T(8,128)(2,1)S(1)}, u32[]{:S(2)}, u32[]{:S(2)}) collective-permute-start(bf16[4,32,1536]{2,1,0:T(8,128)(2,1)S(1)} %pad_maximum_fusion.7.refs_0_), channel_id=1, source_target_pairs={{0,2},{1,3},{2,0},{3,1},{4,6},{5,7},{6,4},{7,5},{8,10},{9,11},{10,... | collective-permute-start | bytes 1179656 | tf_op jit(solution)/shard_map/ppermute | solution.py:575
  39.2 16.5 %collective-permute-start.4 = (bf16[4,32,1536]{2,1,0:T(8,128)(2,1)S(1)}, bf16[4,32,1536]{2,1,0:T(8,128)(2,1)S(1)}, u32[]{:S(2)}, u32[]{:S(2)}) collective-permute-start(bf16[4,32,1536]{2,1,0:T(8,128)(2,1)S(1)} %pad_maximum_fusion.7.refs_0_), channel_id=1, source_target_pairs={{0,4},{1,5},{2,6},{3,7},{4,0},{5,1},{6,2},{7,3},{8,12},{9,13},{10,... | collective-permute-start | bytes 1179656 | tf_op jit(solution)/shard_map/ppermute | solution.py:575
  40.6 16.1 %collective-permute-start.9 = (bf16[4,32,1536]{2,1,0:T(8,128)(2,1)S(1)}, bf16[4,32,1536]{2,1,0:T(8,128)(2,1)S(1)}, u32[]{:S(2)}, u32[]{:S(2)}) collective-permute-start(bf16[4,32,1536]{2,1,0:T(8,128)(2,1)S(1)} %pad_maximum_fusion.7.refs_0_), channel_id=1, source_target_pairs={{0,1},{1,0},{2,3},{3,2},{4,5},{5,4},{6,7},{7,6},{8,9},{9,8},{10,11... | collective-permute-start | bytes 1179656 | tf_op jit(solution)/shard_map/ppermute | solution.py:575
  40.6 19.2 %collective-permute-start.6 = (bf16[4,32,1664]{2,1,0:T(8,128)(2,1)S(1)}, bf16[4,32,1664]{2,1,0:T(8,128)(2,1)S(1)}, u32[]{:S(2)}, u32[]{:S(2)}) collective-permute-start(bf16[4,32,1664]{2,1,0:T(8,128)(2,1)S(1)} %pad_maximum_fusion.6.refs_4_), channel_id=1, source_target_pairs={{0,2},{1,3},{2,0},{3,1},{4,6},{5,7},{6,4},{7,5},{8,10},{9,11},{10,... | collective-permute-start | bytes 1277960 | tf_op jit(solution)/shard_map/ppermute | solution.py:575
  50.7 15.6 %collective-permute-start.8 = (bf16[4,32,1664]{2,1,0:T(8,128)(2,1)S(1)}, bf16[4,32,1664]{2,1,0:T(8,128)(2,1)S(1)}, u32[]{:S(2)}, u32[]{:S(2)}) collective-permute-start(bf16[4,32,1664]{2,1,0:T(8,128)(2,1)S(1)} %collective-permute-done.7.refs_6_), channel_id=1, source_target_pairs={{0,2},{1,3},{2,0},{3,1},{4,6},{5,7},{6,4},{7,5},{8,10},{9,11},{10,... | collective-permute-start | bytes 1277960 | tf_op jit(solution)/shard_map/ppermute | solution.py:575
  55.7 10.5 %collective-permute-start.5 = (bf16[4,32,1536]{2,1,0:T(8,128)(2,1)S(1)}, bf16[4,32,1536]{2,1,0:T(8,128)(2,1)S(1)}, u32[]{:S(2)}, u32[]{:S(2)}) collective-permute-start(bf16[4,32,1536]{2,1,0:T(8,128)(2,1)S(1)} %collective-permute-done.3.refs_1_), channel_id=1, source_target_pairs={{0,4},{1,5},{2,6},{3,7},{4,0},{5,1},{6,2},{7,3},{8,12},{9,13},{10,... | collective-permute-start | bytes 1179656 | tf_op jit(solution)/shard_map/ppermute | solution.py:575
  56.7 10.0 %collective-permute-start.10 = (bf16[4,32,1536]{2,1,0:T(8,128)(2,1)S(1)}, bf16[4,32,1536]{2,1,0:T(8,128)(2,1)S(1)}, u32[]{:S(2)}, u32[]{:S(2)}) collective-permute-start(bf16[4,32,1536]{2,1,0:T(8,128)(2,1)S(1)} %collective-permute-done.3.refs_1_), channel_id=1, source_target_pairs={{0,1},{1,0},{2,3},{3,2},{4,5},{5,4},{6,7},{7,6},{8,9},{9,8},{10,11... | collective-permute-start | bytes 1179656 | tf_op jit(solution)/shard_map/ppermute | solution.py:575
  69.2 26.0 %collective-permute-start.17 = (bf16[512,1024]{1,0:T(8,128)(2,1)S(1)}, bf16[512,1024]{1,0:T(8,128)(2,1)S(1)}, u32[]{:S(2)}, u32[]{:S(2)}) collective-permute-start(bf16[512,1024]{1,0:T(8,128)(2,1)S(1)} %copy-done.4), channel_id=1, source_target_pairs={{0,2},{1,3},{2,0},{3,1},{4,6},{5,7},{6,4},{7,5},{8,10},{9,11},{10,... | collective-permute-start | bytes 3145736 | tf_op jit(solution)/shard_map/ppermute | solution.py:575
  71.3 24.9 %collective-permute-start.18 = (bf16[512,1024]{1,0:T(8,128)(2,1)S(1)}, bf16[512,1024]{1,0:T(8,128)(2,1)S(1)}, u32[]{:S(2)}, u32[]{:S(2)}) collective-permute-start(bf16[512,1024]{1,0:T(8,128)(2,1)S(1)} %copy-done.4), channel_id=1, source_target_pairs={{0,4},{1,5},{2,6},{3,7},{4,0},{5,1},{6,2},{7,3},{8,12},{9,13},{10,... | collective-permute-start | bytes 3145736 | tf_op jit(solution)/shard_map/ppermute | solution.py:575
  96.2 25.1 %collective-permute-start.19 = (bf16[528,1024]{1,0:T(8,128)(2,1)}, bf16[528,1024]{1,0:T(8,128)(2,1)S(1)}, u32[]{:S(2)}, u32[]{:S(2)}) collective-permute-start(bf16[528,1024]{1,0:T(8,128)(2,1)} %get-tuple-element.176.refs_8_.refs_6_), channel_id=1, source_target_pairs={{0,2},{1,3},{2,0},{3,1},{4,6},{5,7},{6,4},{7,5},{8,10},{9,11},{10,... | collective-permute-start | bytes 3244040 | tf_op jit(solution)/shard_map/ppermute | solution.py:575
  96.6 25.1 %collective-permute-start.20 = (bf16[528,1024]{1,0:T(8,128)(2,1)}, bf16[528,1024]{1,0:T(8,128)(2,1)S(1)}, u32[]{:S(2)}, u32[]{:S(2)}) collective-permute-start(bf16[528,1024]{1,0:T(8,128)(2,1)} %get-tuple-element.176.refs_8_.refs_6_), channel_id=1, source_target_pairs={{0,4},{1,5},{2,6},{3,7},{4,0},{5,1},{6,2},{7,3},{8,12},{9,13},{10,... | collective-permute-start | bytes 3244040 | tf_op jit(solution)/shard_map/ppermute | solution.py:575
  97.9 23.8 %collective-permute-start.21 = (bf16[528,1024]{1,0:T(8,128)(2,1)}, bf16[528,1024]{1,0:T(8,128)(2,1)}, u32[]{:S(2)}, u32[]{:S(2)}) collective-permute-start(bf16[528,1024]{1,0:T(8,128)(2,1)} %get-tuple-element.176.refs_8_.refs_6_), channel_id=1, source_target_pairs={{0,1},{1,0},{2,3},{3,2},{4,5},{5,4},{6,7},{7,6},{8,9},{9,8},{10,11... | collective-permute-start | bytes 3244040 | tf_op jit(solution)/shard_map/ppermute | solution.py:575
  121.9 23.4 %collective-permute-start.23 = (bf16[512,1024]{1,0:T(8,128)(2,1)S(1)}, bf16[512,1024]{1,0:T(8,128)(2,1)S(1)}, u32[]{:S(2)}, u32[]{:S(2)}) collective-permute-start(bf16[512,1024]{1,0:T(8,128)(2,1)S(1)} %pad_maximum_fusion.3), channel_id=1, source_target_pairs={{0,2},{1,3},{2,0},{3,1},{4,6},{5,7},{6,4},{7,5},{8,10},{9,11},{10,... | collective-permute-start | bytes 3145736 | tf_op jit(solution)/shard_map/ppermute | solution.py:575
  123.5 24.5 %collective-permute-start.24 = (bf16[528,1024]{1,0:T(8,128)(2,1)S(1)}, bf16[528,1024]{1,0:T(8,128)(2,1)S(1)}, u32[]{:S(2)}, u32[]{:S(2)}) collective-permute-start(bf16[528,1024]{1,0:T(8,128)(2,1)S(1)} %pad_maximum_fusion.2), channel_id=1, source_target_pairs={{0,4},{1,5},{2,6},{3,7},{4,0},{5,1},{6,2},{7,3},{8,12},{9,13},{10,... | collective-permute-start | bytes 3244040 | tf_op jit(solution)/shard_map/ppermute | solution.py:575
  124.8 23.1 %collective-permute-start.25 = (bf16[528,1024]{1,0:T(8,128)(2,1)S(1)}, bf16[528,1024]{1,0:T(8,128)(2,1)S(1)}, u32[]{:S(2)}, u32[]{:S(2)}) collective-permute-start(bf16[528,1024]{1,0:T(8,128)(2,1)S(1)} %collective-permute-done.19.refs_4_), channel_id=1, source_target_pairs={{0,1},{1,0},{2,3},{3,2},{4,5},{5,4},{6,7},{7,6},{8,9},{9,8},{10,11... | collective-permute-start | bytes 3244040 | tf_op jit(solution)/shard_map/ppermute | solution.py:575
  124.9 23.1 %collective-permute-start.27 = (bf16[528,1024]{1,0:T(8,128)(2,1)S(1)}, bf16[528,1024]{1,0:T(8,128)(2,1)S(1)}, u32[]{:S(2)}, u32[]{:S(2)}) collective-permute-start(bf16[528,1024]{1,0:T(8,128)(2,1)S(1)} %collective-permute-done.20.refs_10_), channel_id=1, source_target_pairs={{0,1},{1,0},{2,3},{3,2},{4,5},{5,4},{6,7},{7,6},{8,9},{9,8},{10,11... | collective-permute-start | bytes 3244040 | tf_op jit(solution)/shard_map/ppermute | solution.py:575
  125.4 20.0 %collective-permute-start.26 = (bf16[512,1024]{1,0:T(8,128)(2,1)S(1)}, bf16[512,1024]{1,0:T(8,128)(2,1)S(1)}, u32[]{:S(2)}, u32[]{:S(2)}) collective-permute-start(bf16[512,1024]{1,0:T(8,128)(2,1)S(1)} %collective-permute-done.17.refs_6_), channel_id=1, source_target_pairs={{0,1},{1,0},{2,3},{3,2},{4,5},{5,4},{6,7},{7,6},{8,9},{9,8},{10,11... | collective-permute-start | bytes 3145736 | tf_op jit(solution)/shard_map/ppermute | solution.py:575
  226.4 19.0 %collective-permute-start.36 = (bf16[512,1024]{1,0:T(8,128)(2,1)}, bf16[512,1024]{1,0:T(8,128)(2,1)}, u32[]{:S(2)}, u32[]{:S(2)}) collective-permute-start(bf16[512,1024]{1,0:T(8,128)(2,1)} %get-tuple-element.219), channel_id=1, source_target_pairs={{0,1},{1,0},{2,3},{3,2},{4,5},{5,4},{6,7},{7,6},{8,9},{9,8},{10,11... | collective-permute-start | bytes 3145736 | tf_op jit(solution)/shard_map/ppermute | solution.py:575
  226.6 18.9 %collective-permute-start.37 = (bf16[512,1024]{1,0:T(8,128)(2,1)}, bf16[512,1024]{1,0:T(8,128)(2,1)}, u32[]{:S(2)}, u32[]{:S(2)}) collective-permute-start(bf16[512,1024]{1,0:T(8,128)(2,1)} %get-tuple-element.220), channel_id=1, source_target_pairs={{0,1},{1,0},{2,3},{3,2},{4,5},{5,4},{6,7},{7,6},{8,9},{9,8},{10,11... | collective-permute-start | bytes 3145736 | tf_op jit(solution)/shard_map/ppermute | solution.py:575
  226.9 18.6 %collective-permute-start.38 = (bf16[512,1024]{1,0:T(8,128)(2,1)}, bf16[512,1024]{1,0:T(8,128)(2,1)}, u32[]{:S(2)}, u32[]{:S(2)}) collective-permute-start(bf16[512,1024]{1,0:T(8,128)(2,1)} %get-tuple-element.221), channel_id=1, source_target_pairs={{0,1},{1,0},{2,3},{3,2},{4,5},{5,4},{6,7},{7,6},{8,9},{9,8},{10,11... | collective-permute-start | bytes 3145736 | tf_op jit(solution)/shard_map/ppermute | solution.py:575
  227.1 18.4 %collective-permute-start.35 = (bf16[272,1024]{1,0:T(8,128)(2,1)S(1)}, bf16[272,1024]{1,0:T(8,128)(2,1)}, u32[]{:S(2)}, u32[]{:S(2)}) collective-permute-start(bf16[272,1024]{1,0:T(8,128)(2,1)S(1)} %add_convert_fusion.6), channel_id=1, source_target_pairs={{0,4},{1,5},{2,6},{3,7},{4,0},{5,1},{6,2},{7,3},{8,12},{9,13},{10,... | collective-permute-start | bytes 1671176 | tf_op jit(solution)/shard_map/ppermute | solution.py:575
  228.3 17.1 %collective-permute-start.34 = (bf16[256,1024]{1,0:T(8,128)(2,1)}, bf16[256,1024]{1,0:T(8,128)(2,1)}, u32[]{:S(2)}, u32[]{:S(2)}) collective-permute-start(bf16[256,1024]{1,0:T(8,128)(2,1)} %add_convert_fusion.8), channel_id=1, source_target_pairs={{0,2},{1,3},{2,0},{3,1},{4,6},{5,7},{6,4},{7,5},{8,10},{9,11},{10,... | collective-permute-start | bytes 1572872 | tf_op jit(solution)/shard_map/ppermute | solution.py:575
  245.5 125.2 %reduce-scatter.5.cloned.1.call-start = ((), (), s32[]{:S(2)}) async-start(), calls=%async_computation.6 | async-start | bytes 5242880 | tf_op jit(solution)/shard_map/reduce_scatter | solution.py:718
  250.6 30.4 %collective-permute-start.39 = (bf16[528,1024]{1,0:T(8,128)(2,1)}, bf16[528,1024]{1,0:T(8,128)(2,1)S(1)}, u32[]{:S(2)}, u32[]{:S(2)}) collective-permute-start(bf16[528,1024]{1,0:T(8,128)(2,1)} %add_convert_fusion.1), channel_id=1, source_target_pairs={{0,2},{1,3},{2,0},{3,1},{4,6},{5,7},{6,4},{7,5},{8,10},{9,11},{10,... | collective-permute-start | bytes 3244040 | tf_op jit(solution)/shard_map/ppermute | solution.py:575
  251.5 29.5 %collective-permute-start.40 = (bf16[528,1024]{1,0:T(8,128)(2,1)}, bf16[528,1024]{1,0:T(8,128)(2,1)}, u32[]{:S(2)}, u32[]{:S(2)}) collective-permute-start(bf16[528,1024]{1,0:T(8,128)(2,1)} %add_convert_fusion), channel_id=1, source_target_pairs={{0,4},{1,5},{2,6},{3,7},{4,0},{5,1},{6,2},{7,3},{8,12},{9,13},{10,... | collective-permute-start | bytes 3244040 | tf_op jit(solution)/shard_map/ppermute | solution.py:575
  252.3 28.7 %collective-permute-start.41 = (bf16[528,1024]{1,0:T(8,128)(2,1)}, bf16[528,1024]{1,0:T(8,128)(2,1)}, u32[]{:S(2)}, u32[]{:S(2)}) collective-permute-start(bf16[528,1024]{1,0:T(8,128)(2,1)} %get-tuple-element.268), channel_id=1, source_target_pairs={{0,1},{1,0},{2,3},{3,2},{4,5},{5,4},{6,7},{7,6},{8,9},{9,8},{10,11... | collective-permute-start | bytes 3244040 | tf_op jit(solution)/shard_map/ppermute | solution.py:575
  252.3 28.7 %collective-permute-start.42 = (bf16[512,1024]{1,0:T(8,128)(2,1)S(1)}, bf16[512,1024]{1,0:T(8,128)(2,1)}, u32[]{:S(2)}, u32[]{:S(2)}) collective-permute-start(bf16[512,1024]{1,0:T(8,128)(2,1)S(1)} %get-tuple-element.269), channel_id=1, source_target_pairs={{0,1},{1,0},{2,3},{3,2},{4,5},{5,4},{6,7},{7,6},{8,9},{9,8},{10,11... | collective-permute-start | bytes 3145736 | tf_op jit(solution)/shard_map/ppermute | solution.py:575
  283.5 37.4 %collective-permute-start.43 = (bf16[512,1024]{1,0:T(8,128)(2,1)}, bf16[512,1024]{1,0:T(8,128)(2,1)}, u32[]{:S(2)}, u32[]{:S(2)}) collective-permute-start(bf16[512,1024]{1,0:T(8,128)(2,1)} %get-tuple-element.301), channel_id=1, source_target_pairs={{0,2},{1,3},{2,0},{3,1},{4,6},{5,7},{6,4},{7,5},{8,10},{9,11},{10,... | collective-permute-start | bytes 3145736 | tf_op jit(solution)/shard_map/ppermute | solution.py:575
  284.5 36.4 %collective-permute-start.44 = (bf16[512,1024]{1,0:T(8,128)(2,1)}, bf16[512,1024]{1,0:T(8,128)(2,1)}, u32[]{:S(2)}, u32[]{:S(2)}) collective-permute-start(bf16[512,1024]{1,0:T(8,128)(2,1)} %get-tuple-element.302), channel_id=1, source_target_pairs={{0,4},{1,5},{2,6},{3,7},{4,0},{5,1},{6,2},{7,3},{8,12},{9,13},{10,... | collective-permute-start | bytes 3145736 | tf_op jit(solution)/shard_map/ppermute | solution.py:575
  285.8 35.0 %collective-permute-start.45 = (bf16[256,1024]{1,0:T(8,128)(2,1)}, bf16[256,1024]{1,0:T(8,128)(2,1)}, u32[]{:S(2)}, u32[]{:S(2)}) collective-permute-start(bf16[256,1024]{1,0:T(8,128)(2,1)} %get-tuple-element.303), channel_id=1, source_target_pairs={{0,6},{1,7},{2,4},{3,5},{4,2},{5,3},{6,0},{7,1},{8,14},{9,15},{10,... | collective-permute-start | bytes 1572872 | tf_op jit(solution)/shard_map/ppermute | solution.py:575
  320.8 13.9 %collective-permute-start.46 = (bf16[256,1024]{1,0:T(8,128)(2,1)S(1)}, bf16[256,1024]{1,0:T(8,128)(2,1)S(1)}, u32[]{:S(2)}, u32[]{:S(2)}) collective-permute-start(bf16[256,1024]{1,0:T(8,128)(2,1)S(1)} %get-tuple-element.308), channel_id=1, source_target_pairs={{0,6},{1,7},{2,4},{3,5},{4,2},{5,3},{6,0},{7,1},{8,14},{9,15},{10,... | collective-permute-start | bytes 1572872 | tf_op jit(solution)/shard_map/ppermute | solution.py:575
  322.5 13.6 %collective-permute-start.48 = (bf16[8,32,1536]{2,1,0:T(8,128)(2,1)}, bf16[8,32,1536]{2,1,0:T(8,128)(2,1)S(1)}, u32[]{:S(2)}, u32[]{:S(2)}) collective-permute-start(bf16[8,32,1536]{2,1,0:T(8,128)(2,1)} %get-tuple-element.313), channel_id=1, source_target_pairs={{0,1},{1,0},{2,3},{3,2},{4,5},{5,4},{6,7},{7,6},{8,9},{9,8},{10,11... | collective-permute-start | bytes 2359304 | tf_op jit(solution)/shard_map/ppermute | solution.py:575
  322.5 16.1 %collective-permute-start.47 = (bf16[8,32,1536]{2,1,0:T(8,128)(2,1)}, bf16[8,32,1536]{2,1,0:T(8,128)(2,1)S(1)}, u32[]{:S(2)}, u32[]{:S(2)}) collective-permute-start(bf16[8,32,1536]{2,1,0:T(8,128)(2,1)} %get-tuple-element.311), channel_id=1, source_target_pairs={{0,1},{1,0},{2,3},{3,2},{4,5},{5,4},{6,7},{7,6},{8,9},{9,8},{10,11... | collective-permute-start | bytes 2359304 | tf_op jit(solution)/shard_map/ppermute | solution.py:575
  323.0 13.3 %collective-permute-start.49 = (bf16[8,32,1664]{2,1,0:T(8,128)(2,1)}, bf16[8,32,1664]{2,1,0:T(8,128)(2,1)S(1)}, u32[]{:S(2)}, u32[]{:S(2)}) collective-permute-start(bf16[8,32,1664]{2,1,0:T(8,128)(2,1)} %get-tuple-element.315), channel_id=1, source_target_pairs={{0,1},{1,0},{2,3},{3,2},{4,5},{5,4},{6,7},{7,6},{8,9},{9,8},{10,11... | collective-permute-start | bytes 2555912 | tf_op jit(solution)/shard_map/ppermute | solution.py:575
  323.0 16.6 %collective-permute-start.52 = (bf16[8,32,1664]{2,1,0:T(8,128)(2,1)}, bf16[8,32,1664]{2,1,0:T(8,128)(2,1)S(1)}, u32[]{:S(2)}, u32[]{:S(2)}) collective-permute-start(bf16[8,32,1664]{2,1,0:T(8,128)(2,1)} %get-tuple-element.318), channel_id=1, source_target_pairs={{0,1},{1,0},{2,3},{3,2},{4,5},{5,4},{6,7},{7,6},{8,9},{9,8},{10,11... | collective-permute-start | bytes 2555912 | tf_op jit(solution)/shard_map/ppermute | solution.py:575
  337.5 17.7 %collective-permute-start.50 = (bf16[8,32,1536]{2,1,0:T(8,128)(2,1)S(1)}, bf16[8,32,1536]{2,1,0:T(8,128)(2,1)S(1)}, u32[]{:S(2)}, u32[]{:S(2)}) collective-permute-start(bf16[8,32,1536]{2,1,0:T(8,128)(2,1)S(1)} %add_convert_fusion.4), channel_id=1, source_target_pairs={{0,2},{1,3},{2,0},{3,1},{4,6},{5,7},{6,4},{7,5},{8,10},{9,11},{10,... | collective-permute-start | bytes 2359304 | tf_op jit(solution)/shard_map/ppermute | solution.py:575
  338.8 21.4 %collective-permute-start.53 = (bf16[8,32,1664]{2,1,0:T(8,128)(2,1)S(1)}, bf16[8,32,1664]{2,1,0:T(8,128)(2,1)S(1)}, u32[]{:S(2)}, u32[]{:S(2)}) collective-permute-start(bf16[8,32,1664]{2,1,0:T(8,128)(2,1)S(1)} %add_convert_fusion.3), channel_id=1, source_target_pairs={{0,4},{1,5},{2,6},{3,7},{4,0},{5,1},{6,2},{7,3},{8,12},{9,13},{10,... | collective-permute-start | bytes 2555912 | tf_op jit(solution)/shard_map/ppermute | solution.py:575
  355.3 10.9 %collective-permute-start.51 = (bf16[4,32,1536]{2,1,0:T(8,128)(2,1)S(1)}, bf16[4,32,1536]{2,1,0:T(8,128)(2,1)S(1)}, u32[]{:S(2)}, u32[]{:S(2)}) collective-permute-start(bf16[4,32,1536]{2,1,0:T(8,128)(2,1)S(1)} %add_convert_fusion.13), channel_id=1, source_target_pairs={{0,4},{1,5},{2,6},{3,7},{4,0},{5,1},{6,2},{7,3},{8,12},{9,13},{10,... | collective-permute-start | bytes 1179656 | tf_op jit(solution)/shard_map/ppermute | solution.py:575
  375.5 16.2 %collective-permute-start.56 = (bf16[32,3200]{1,0:T(8,128)(2,1)}, bf16[32,3200]{1,0:T(8,128)(2,1)}, u32[]{:S(2)}, u32[]{:S(2)}) collective-permute-start(bf16[32,3200]{1,0:T(8,128)(2,1)} %get-tuple-element.371), channel_id=1, source_target_pairs={{0,16},{1,17},{2,18},{3,19},{4,20},{5,21},{6,22},{7,23},{8,24},{9,... | collective-permute-start | bytes 614408 | tf_op jit(solution)/shard_map/ppermute | solution.py:575
  378.4 13.4 %collective-permute-start.57 = (bf16[32,3200]{1,0:T(8,128)(2,1)}, bf16[32,3200]{1,0:T(8,128)(2,1)}, u32[]{:S(2)}, u32[]{:S(2)}) collective-permute-start(bf16[32,3200]{1,0:T(8,128)(2,1)} %get-tuple-element.370), channel_id=1, source_target_pairs={{0,24},{1,25},{2,26},{3,27},{4,28},{5,29},{6,30},{7,31},{8,16},{9,... | collective-permute-start | bytes 614408 | tf_op jit(solution)/shard_map/ppermute | solution.py:575
  379.6 24.5 %all-to-all-start.1 = ((bf16[8,6,32,512]{3,2,1,0:T(8,128)(2,1)}), bf16[8,6,32,512]{3,2,1,0:T(8,128)(2,1)S(1)}, u32[]{:S(2)}, u32[]{:S(2)}) async-start(bf16[8,6,32,512]{3,2,1,0:T(8,128)(2,1)} %pad_maximum_fusion.1), calls=%async_computation.3 | async-start | bytes 3145728 | tf_op jit(solution)/shard_map/all_to_all | solution.py:773
  (66 other events, 593.5 us)
Sparse Core Ops, SparseCore 0:
  37.6 114.7 all-gather.1
  245.6 43.7 reduce-scatter.2
  291.9 76.1 reduce-scatter.4
